TPU v7x, 128 devices: a whole 4x4x4 slice. The times are simulated.
128 devices in a mesh: wide: 16 (over x, y_lo, core), narrow: 8 (over z, y_hi).
Axes of the slice: x: 4, y: 4 (y_hi: 2, y_lo: 2; y = y_hi * 2 + y_lo), z: 4, core: 2. Of those that a mesh axis runs over, the one named last changes fastest.
Arguments:
- node_features: bfloat16 [8192, 25, 128], P(('wide', 'narrow')), may hold values from -6 to 6
- frames: bfloat16 [8192, 48, 165], P(('wide', 'narrow')), may hold values from -6 to 6
- radial: bfloat16 [8192, 48, 128], P(('wide', 'narrow')), may hold values from 0.29882812 to 3
- neighbours: int32 [8192, 48], P(('wide', 'narrow')), may hold values from 0 to 8191, as said below
- counts: int32 [8192], P(('wide', 'narrow')), may hold values from 16 to 48
- coefficients: float32 [32], P('wide'), may hold values from 0.05 to 0.5
- w_zero: bfloat16 [32, 640, 640], P('wide'), may hold values from -0.25 to 0.25
- w_one: bfloat16 [32, 2, 512, 512], P('wide'), may hold values from -0.1875 to 0.1875
- w_two: bfloat16 [32, 2, 384, 384], P('wide'), may hold values from -0.21875 to 0.21875
- w_three: bfloat16 [32, 2, 256, 256], P('wide'), may hold values from -0.25 to 0.25
- w_four: bfloat16 [32, 2, 128, 128], P('wide'), may hold values from -0.375 to 0.375
Outputs:
- conv_out: float32 [8192, 25, 128], P(('wide', 'narrow'))
Inputs may be any that keep to these rules, and one draw needn't show every extreme that they name: `neighbours`: each neighbour of an atom lies in the atom's own aligned block of 64 atoms or in one of the two cyclically adjacent blocks. `counts`: slots at or beyond an atom's count are padding and carry arbitrary indices.
All inputs are finite; a program needn't handle non-finite values.
Results may differ from a plain program's by a relative error of at most 0.02.
Values may be sent and summed in bfloat16 or wider, within the bound.
No kernel may reach another device: no remote copies, remote signals or barrier semaphores. Data moves between devices by JAX's collectives and lax.ppermute only.
A program may use at most 192 MiB of HBM per device.

v0:
```python
import jax
import jax.numpy as jnp
import numpy as np
from jax import lax
from jax.sharding import PartitionSpec as P


def with_halo(x, sides, width):
    edges = {}
    for axis, dim in sides:
        size, length = (lax.axis_size(axis), x.shape[dim])
        up = [(i, (i + 1) % size) for i in range(size)]
        last = lax.slice_in_dim(x, length - width, length, axis=dim)
        first = lax.slice_in_dim(x, 0, width, axis=dim)
        edges[dim] = (
            lax.ppermute(last, axis, up),
            lax.ppermute(first, axis, [(b, a) for a, b in up]),
        )
    done = []
    for _, dim in sides:
        low, high = edges[dim]
        around = [(width, width) if d in done else (0, 0) for d in range(x.ndim)]
        x = jnp.concatenate([jnp.pad(low, around), x, jnp.pad(high, around)], axis=dim)
        done.append(dim)
    return x


def cut_along(x, dim, length):
    before, after = (x.shape[:dim], x.shape[dim + 1 :])
    return jnp.moveaxis(x.reshape(*before, length, -1, *after), dim, 0)


def sum_at_owner(x, axis, dim):
    length = lax.axis_size(axis)
    tiles = lax.all_to_all(cut_along(x, dim, length), axis, 0, 0, tiled=True)
    return jnp.sum(tiles.astype(jnp.float32), axis=0)


def joined_along(tiles, dim):
    shape = list(tiles.shape[1:])
    shape[dim] *= tiles.shape[0]
    return jnp.moveaxis(tiles, 0, dim).reshape(shape)


def gather_together(arrays, axis, dims):
    ravelled = jnp.concatenate([a.reshape(-1) for a in arrays])
    lines, at, finished = (lax.all_gather(ravelled, axis), 0, [])
    for a, dim in zip(arrays, dims):
        tiles = lines[:, at : at + a.size].reshape(-1, *a.shape)
        finished.append(joined_along(tiles, dim))
        at += a.size
    return tuple(finished)


def grouped_order():
    order_list = [degree * degree + degree for degree in range(5)]
    for order in range(1, 5):
        order_list += [degree * degree + degree + order for degree in range(order, 5)]
        order_list += [degree * degree + degree - order for degree in range(order, 5)]
    return order_list


def frame_table():
    position = np.zeros(25, np.int64)
    for place, component in enumerate(grouped_order()):
        position[component] = place
    table = np.zeros((165, 625), np.float32)
    offset = 0
    for degree in range(5):
        order_size = 2 * degree + 1
        for row in range(order_size):
            for column in range(order_size):
                target = position[degree * degree + row] * 25 + degree * degree + column
                table[offset + row * order_size + column, target] = 1.0
        offset += order_size * order_size
    return table


def block_weights(merged):
    result = [merged[0]]
    for order in range(1, 5):
        real_part = merged[order][0]
        imag_part = merged[order][1]
        upper = jnp.concatenate([real_part, imag_part], axis=1)
        lower = jnp.concatenate([-imag_part, real_part], axis=1)
        result.append(jnp.concatenate([upper, lower], axis=0))
    return result


def messages(gathered, frames, radial, weights, table):
    row_count = gathered.shape[0]
    channels = gathered.shape[2]
    dense = jnp.dot(frames, table, preferred_element_type=jnp.float32).reshape(row_count, 25, 25)
    dense_half = dense.astype(jnp.bfloat16)
    rotated = jnp.einsum("rpq,rqc->rpc", dense_half, gathered, preferred_element_type=jnp.float32)
    rotated = (rotated * radial.astype(jnp.float32)[:, None, :]).astype(jnp.bfloat16)
    pieces = []
    start = 0
    for order in range(5):
        width = 5 if order == 0 else 2 * (5 - order)
        inputs = rotated[:, start : start + width, :].reshape(row_count, width * channels)
        output = jnp.dot(inputs, weights[order], preferred_element_type=jnp.float32)
        pieces.append(output.reshape(row_count, width, channels))
        start += width
    mixed = jnp.concatenate(pieces, axis=1)
    scalar = mixed[:, 0:1, :]
    gated = jnp.concatenate([jax.nn.silu(scalar), mixed[:, 1:, :] * jax.nn.sigmoid(scalar)], axis=1)
    return jnp.einsum(
        "rqp,rqc->rpc",
        dense,
        gated,
        precision=lax.Precision.HIGHEST,
        preferred_element_type=jnp.float32,
    )


def body(
    node_features,
    frames,
    radial,
    neighbours,
    counts,
    coefficients,
    w_zero,
    w_one,
    w_two,
    w_three,
    w_four,
):
    atoms_here = node_features.shape[0]
    channels = node_features.shape[2]
    slot_total = neighbours.shape[1]
    extended = with_halo(node_features, ((("wide", "narrow"), 0),), atoms_here)

    def combine(weights):
        summed_total = coefficients[0] * weights[0].astype(jnp.float32)
        summed_total = summed_total + coefficients[1] * weights[1].astype(jnp.float32)
        return summed_total.astype(jnp.bfloat16)

    partial_zero = combine(w_zero)[None]
    partial_one = combine(w_one)
    partial_two = combine(w_two)
    partial_three = combine(w_three)
    partial_four = combine(w_four)
    shares = (
        sum_at_owner(partial_zero, "wide", 1),
        sum_at_owner(partial_one, "wide", 1),
        sum_at_owner(partial_two, "wide", 1),
        sum_at_owner(partial_three, "wide", 1),
        sum_at_owner(partial_four, "wide", 1),
    )
    merged_all = gather_together(
        (
            shares[0].astype(jnp.bfloat16),
            shares[1].astype(jnp.bfloat16),
            shares[2].astype(jnp.bfloat16),
            shares[3].astype(jnp.bfloat16),
            shares[4].astype(jnp.bfloat16),
        ),
        "wide",
        (1, 1, 1, 1, 1),
    )
    merged = (merged_all[0][0], merged_all[1], merged_all[2], merged_all[3], merged_all[4])
    weights = block_weights(merged)
    table = jnp.asarray(frame_table()).astype(jnp.bfloat16)
    slot_group = 8
    for candidate in range(8, slot_total + 1, 8):
        if slot_total % candidate == 0 and atoms_here * candidate <= 1536:
            slot_group = candidate
    block_start = lax.axis_index(("wide", "narrow")) * atoms_here
    atoms_total = atoms_here * lax.axis_size(("wide", "narrow"))
    local_index = (neighbours - block_start + atoms_here) % atoms_total
    live_slots = (lax.broadcasted_iota(jnp.int32, neighbours.shape, 1) < counts[:, None]).astype(
        jnp.float32
    )

    def accumulate(carried, group_index):
        first_slot = group_index * slot_group
        index_block = lax.dynamic_slice_in_dim(local_index, first_slot, slot_group, 1).reshape(-1)
        frame_rows = lax.dynamic_slice_in_dim(frames, first_slot, slot_group, 1).reshape(
            -1, frames.shape[2]
        )
        radial_rows = lax.dynamic_slice_in_dim(radial, first_slot, slot_group, 1).reshape(
            -1, channels
        )
        live_block = lax.dynamic_slice_in_dim(live_slots, first_slot, slot_group, 1)
        gathered = jnp.take(extended, index_block, axis=0)
        result = messages(gathered, frame_rows, radial_rows, weights, table).reshape(
            atoms_here, slot_group, 25, channels
        )
        return (carried + jnp.sum(result * live_block[:, :, None, None], axis=1), None)

    initial = jnp.zeros((atoms_here, 25, channels), jnp.float32)
    summed_out, ignored = lax.scan(accumulate, initial, jnp.arange(slot_total // slot_group))
    return summed_out / jnp.sqrt(counts.astype(jnp.float32))[:, None, None]


def solution(mesh):
    in_specs = (
        P(("wide", "narrow"), None, None),
        P(("wide", "narrow"), None, None),
        P(("wide", "narrow"), None, None),
        P(("wide", "narrow"), None),
        P(("wide", "narrow")),
        P("wide"),
        P("wide", None, None),
        P("wide", None, None, None),
        P("wide", None, None, None),
        P("wide", None, None, None),
        P("wide", None, None, None),
    )
    out_specs = P(("wide", "narrow"), None, None)
    return jax.shard_map(body, mesh=mesh, in_specs=in_specs, out_specs=out_specs, check_vma=False)
```

profile of v0, /device:TPU:1, one launch (start us, length us, event | category | flops | bytes accessed | tf_op | source)
XLA Modules:
  0.0 532.4 jit_solution(12447645997418914861)
XLA Ops:
  10.7 6.8 %all-to-all-start.4 = ((bf16[16,2,8,128]{3,2,1,0:T(8,128)(2,1)}), bf16[16,2,8,128]{3,2,1,0:T(8,128)(2,1)S(1)}, u32[]{:S(2)}, u32[]{:S(2)}) async-start(bf16[16,2,8,128]{3,2,1,0:T(8,128)(2,1)} %copy.86), calls=%async_computation.4 | async-start | bytes 131072 | tf_op jit(solution)/shard_map/all_to_all | solution.py:35
  17.5 2.4 add_convert_fusion.3
  20.7 2.7 all-to-all-done.4
  23.4 3.7 all-to-all-start.3
  29.5 5.1 all-to-all-done.3
  34.6 3.8 all-to-all-start.2
  38.4 2.5 add_convert_fusion.1
  40.8 7.8 %all-to-all-done.2 = bf16[16,2,24,384]{3,2,1,0:T(8,128)(2,1)S(1)} async-done(((bf16[16,2,24,384]{3,2,1,0:T(8,128)(2,1)}), bf16[16,2,24,384]{3,2,1,0:T(8,128)(2,1)S(1)}, u32[]{:S(2)}, u32[]{:S(2)}) %all-to-all-start.2) | async-done | bytes 589856 | tf_op jit(solution)/shard_map/all_to_all | solution.py:35
  48.6 4.9 all-to-all-start
  53.5 3.2 add_convert_fusion
  57.7 8.9 %all-to-all-done = bf16[16,1,40,640]{3,2,1,0:T(8,128)(2,1)S(1)} async-done(((bf16[16,1,40,640]{3,2,1,0:T(8,128)(2,1)}), bf16[16,1,40,640]{3,2,1,0:T(8,128)(2,1)S(1)}, u32[]{:S(2)}, u32[]{:S(2)}) %all-to-all-start) | async-done | bytes 819232 | tf_op jit(solution)/shard_map/all_to_all | solution.py:35
  66.6 4.5 all-to-all-start.1
  71.6 15.3 %all-to-all-done.1 = bf16[16,2,32,512]{3,2,1,0:T(8,128)(2,1)S(1)} async-done(((bf16[16,2,32,512]{3,2,1,0:T(8,128)(2,1)}), bf16[16,2,32,512]{3,2,1,0:T(8,128)(2,1)S(1)}, u32[]{:S(2)}, u32[]{:S(2)}) %all-to-all-start.1) | async-done | bytes 1048608 | tf_op jit(solution)/shard_map/all_to_all | solution.py:35
  88.2 2.7 collective-permute-start
  90.9 4.3 collective-permute-start.1
  99.2 16.3 %collective-permute-done = bf16[64,25,128]{2,1,0:T(8,128)(2,1)S(1)} collective-permute-done((bf16[64,25,128]{2,1,0:T(8,128)(2,1)S(1)}, bf16[64,25,128]{2,1,0:T(8,128)(2,1)S(1)}, u32[]{:S(2)}, u32[]{:S(2)}) %collective-permute-start) | collective-permute-done | bytes 409632 | tf_op jit(solution)/shard_map/ppermute | solution.py:16
  115.4 12.5 %collective-permute-done.1 = bf16[64,25,128]{2,1,0:T(8,128)(2,1)S(1)} collective-permute-done((bf16[64,25,128]{2,1,0:T(8,128)(2,1)S(1)}, bf16[64,25,128]{2,1,0:T(8,128)(2,1)S(1)}, u32[]{:S(2)}, u32[]{:S(2)}) %collective-permute-start.1) | collective-permute-done | bytes 409632 | tf_op jit(solution)/shard_map/ppermute | solution.py:17
  128.2 3.6 reshape.236
  146.4 2.3 copy.103
  150.2 2.3 maximum_maximum_fusion.1
  154.2 368.8 %while.12 = (s32[]{:T(128)}, f32[64,25,128]{2,1,0:T(8,128)}, s32[2]{0:T(128)S(1)}, bf16[64,48,165]{2,1,0:T(8,128)(2,1)}, s32[64,48]{1,0:T(8,128)S(1)}, /*index=5...) while((s32[]{:T(128)}, f32[64,25,128]{2,1,0:T(8,128)}, ...), condition=%wide.region_7.8_spmd.clone.clone, body=%wide.region_5.7_spmd.clone.clone.sunk | while | flops 9371582464 | bytes 297363392 | solution.py:194
  156.8 3.8 fusion.70
  160.6 18.6 %copy.127 = bf16[1536,25,25]{2,1,0:T(8,128)(2,1)} copy(bf16[1536,25,25]{0,2,1:T(8,128)(2,1)} %get-tuple-element.386) | data formatting | bytes 3840000 | tf_op jit(solution)/shard_map/while/body/eval_jaxpr/convert_element_type | solution.py:94
  179.4 7.3 %gather_fusion = bf16[1536,25,128]{2,1,0:T(8,128)(2,1)} fusion(bf16[192,25,128]{2,1,0:T(8,128)(2,1)S(1)} %get-tuple-element.432, s32[2048]{0:T(1024)S(1)} %pad_clamp_fusion.2), kind=kCustom, calls=%fused_computation.clone.clone.clone.1 | custom fusion | bytes 19666944 | tf_op jit(solution)/shard_map/while/body/eval_jaxpr/jit(_take)/gather | solution.py:187
  188.0 15.9 %multiply_convert_fusion.2 = bf16[1536,25,128]{2,1,0:T(8,128)(2,1)} fusion(f32[1536,128]{1,0:T(8,128)S(1)} %bitcast_convert_fusion.2, bf16[1536,25,25]{2,1,0:T(8,128)(2,1)} %copy.127, bf16[1536,25,128]{2,1,0:T(8,128)(2,1)} %gather_fusion, pred[1536]{0:T(1024)(128)(4,1)S(1)} %compare_and_fusion.2), kind=kOutput, calls=%fused_computation.5.clone.1 | convolution fusion | flops 260505600 | bytes 22368768 | tf_op jit(solution)/shard_map/while/body/eval_jaxpr/rpq,rqc->rpc/dot_general | solution.py:95
  205.9 2.8 copy.128
  208.7 6.8 %constant_dynamic-update-slice_fusion.7 = (f32[1536,25,128]{2,0,1:T(8,128)}, f32[1536,5,128]{2,0,1:T(8,128)}) fusion(bf16[1536,640,1]{0,1,2:T(8,128)(2,1)} %bitcast.150, bf16[5,128,640]{2,1,0:T(8,128)(2,1)} %bitcast.153), kind=kOutput, calls=%fused_computation.23.clone.1 | convolution fusion | flops 1258291200 | bytes 10649600 | tf_op jit(solution)/shard_map/while/body/eval_jaxpr/dot_general | solution.py:102
  215.5 3.4 slice.213
  218.9 3.3 reshape.284
  222.2 7.4 %convolution_dynamic-update-slice_fusion.8 = f32[1536,25,128]{2,0,1:T(8,128)} fusion(f32[1536,25,128]{2,0,1:T(8,128)} %get-tuple-element.387, bf16[1536,1024,1]{1,0,2:T(8,128)(2,1)} %reshape.284, bf16[8,128,1024]{2,1,0:T(8,128)(2,1)} %bitcast.162), kind=kOutput, calls=%fused_computation.12.clone.1 | convolution fusion | flops 3221225472 | bytes 11534336 | tf_op jit(solution)/shard_map/while/body/eval_jaxpr/dot_general | solution.py:102
  229.7 3.4 slice.214
  233.0 3.0 copy.129
  236.1 6.3 %convolution_dynamic-update-slice_fusion.9 = f32[1536,25,128]{2,0,1:T(8,128)} fusion(f32[1536,25,128]{2,0,1:T(8,128)} %convolution_dynamic-update-slice_fusion.8, bf16[1536,768,1]{0,1,2:T(8,128)(2,1)} %bitcast.152, bf16[6,128,768]{2,1,0:T(8,128)(2,1)} %bitcast.165), kind=kOutput, calls=%fused_computation.13.clone.1 | convolution fusion | flops 1811939328 | bytes 8257536 | tf_op jit(solution)/shard_map/while/body/eval_jaxpr/dot_general | solution.py:102
  242.3 2.3 slice.215
  245.3 3.7 convolution_dynamic-update-slice_fusion.10
  249.0 3.4 slice.216
  255.8 7.1 %slice_multiply_fusion.5 = f32[1536,24,128]{2,0,1:T(8,128)S(1)} fusion(f32[1536,25,128]{2,0,1:T(8,128)} %convolution_dynamic-update-slice_fusion.11, f32[1536,128]{1,0:T(8,128)S(1)} %get-tuple-element.389), kind=kLoop, calls=%fused_computation.7.clone.1 | loop fusion | flops 4718592 | bytes 38535168 | tf_op jit(solution)/shard_map/while/body/eval_jaxpr/mul | solution.py:107
  263.0 7.1 %pad_maximum_fusion.3 = f32[1536,25,128]{2,0,1:T(8,128)} fusion(f32[1536,24,128]{2,0,1:T(8,128)S(1)} %slice_multiply_fusion.5, f32[1536,1,128]{2,0,1:T(8,128)S(1)} %get-tuple-element.390), kind=kLoop, calls=%fused_computation.6.clone.1 | loop fusion | flops 4915200 | bytes 39321600 | tf_op jit(solution)/shard_map/while/body/eval_jaxpr/concatenate | solution.py:107
  270.0 20.9 %copy.126 = f32[1536,25,25]{1,2,0:T(8,128)} copy(f32[1536,25,25]{0,2,1:T(8,128)} %get-tuple-element.385) | data formatting | bytes 7680000 | tf_op jit(solution)/shard_map/while/body/eval_jaxpr/dot_general | solution.py:93
  290.9 40.7 %fusion.72 = f32[1536,25,128]{2,1,0:T(8,128)S(1)} fusion(f32[1536,25,25]{1,2,0:T(8,128)} %copy.126, f32[1536,25,128]{2,0,1:T(8,128)} %pad_maximum_fusion.3), kind=kOutput, calls=%fused_computation.2.clone.1 | convolution fusion | flops 1474560000 | bytes 43161600 | tf_op jit(solution)/shard_map/while/body/eval_jaxpr/rqp,rqc->rpc/dot_general | solution.py:108
  331.7 4.1 multiply_reduce_fusion.2
  335.8 2.5 select_add_fusion.2
  341.0 3.8 fusion.70
  344.8 18.6 %copy.127 = bf16[1536,25,25]{2,1,0:T(8,128)(2,1)} copy(bf16[1536,25,25]{0,2,1:T(8,128)(2,1)} %get-tuple-element.386) | data formatting | bytes 3840000 | tf_op jit(solution)/shard_map/while/body/eval_jaxpr/convert_element_type | solution.py:94
  363.7 7.3 %gather_fusion = bf16[1536,25,128]{2,1,0:T(8,128)(2,1)} fusion(bf16[192,25,128]{2,1,0:T(8,128)(2,1)S(1)} %get-tuple-element.432, s32[2048]{0:T(1024)S(1)} %pad_clamp_fusion.2), kind=kCustom, calls=%fused_computation.clone.clone.clone.1 | custom fusion | bytes 19666944 | tf_op jit(solution)/shard_map/while/body/eval_jaxpr/jit(_take)/gather | solution.py:187
  372.2 15.9 %multiply_convert_fusion.2 = bf16[1536,25,128]{2,1,0:T(8,128)(2,1)} fusion(f32[1536,128]{1,0:T(8,128)S(1)} %bitcast_convert_fusion.2, bf16[1536,25,25]{2,1,0:T(8,128)(2,1)} %copy.127, bf16[1536,25,128]{2,1,0:T(8,128)(2,1)} %gather_fusion, pred[1536]{0:T(1024)(128)(4,1)S(1)} %compare_and_fusion.2), kind=kOutput, calls=%fused_computation.5.clone.1 | convolution fusion | flops 260505600 | bytes 22368768 | tf_op jit(solution)/shard_map/while/body/eval_jaxpr/rpq,rqc->rpc/dot_general | solution.py:95
  390.1 2.8 copy.128
  393.0 6.8 %constant_dynamic-update-slice_fusion.7 = (f32[1536,25,128]{2,0,1:T(8,128)}, f32[1536,5,128]{2,0,1:T(8,128)}) fusion(bf16[1536,640,1]{0,1,2:T(8,128)(2,1)} %bitcast.150, bf16[5,128,640]{2,1,0:T(8,128)(2,1)} %bitcast.153), kind=kOutput, calls=%fused_computation.23.clone.1 | convolution fusion | flops 1258291200 | bytes 10649600 | tf_op jit(solution)/shard_map/while/body/eval_jaxpr/dot_general | solution.py:102
  399.8 3.4 slice.213
  403.1 3.3 reshape.284
  406.5 7.4 %convolution_dynamic-update-slice_fusion.8 = f32[1536,25,128]{2,0,1:T(8,128)} fusion(f32[1536,25,128]{2,0,1:T(8,128)} %get-tuple-element.387, bf16[1536,1024,1]{1,0,2:T(8,128)(2,1)} %reshape.284, bf16[8,128,1024]{2,1,0:T(8,128)(2,1)} %bitcast.162), kind=kOutput, calls=%fused_computation.12.clone.1 | convolution fusion | flops 3221225472 | bytes 11534336 | tf_op jit(solution)/shard_map/while/body/eval_jaxpr/dot_general | solution.py:102
  413.9 3.4 slice.214
  417.3 3.0 copy.129
  420.3 6.3 %convolution_dynamic-update-slice_fusion.9 = f32[1536,25,128]{2,0,1:T(8,128)} fusion(f32[1536,25,128]{2,0,1:T(8,128)} %convolution_dynamic-update-slice_fusion.8, bf16[1536,768,1]{0,1,2:T(8,128)(2,1)} %bitcast.152, bf16[6,128,768]{2,1,0:T(8,128)(2,1)} %bitcast.165), kind=kOutput, calls=%fused_computation.13.clone.1 | convolution fusion | flops 1811939328 | bytes 8257536 | tf_op jit(solution)/shard_map/while/body/eval_jaxpr/dot_general | solution.py:102
  426.6 2.3 slice.215
  429.5 3.7 convolution_dynamic-update-slice_fusion.10
  433.3 3.4 slice.216
  440.1 7.1 %slice_multiply_fusion.5 = f32[1536,24,128]{2,0,1:T(8,128)S(1)} fusion(f32[1536,25,128]{2,0,1:T(8,128)} %convolution_dynamic-update-slice_fusion.11, f32[1536,128]{1,0:T(8,128)S(1)} %get-tuple-element.389), kind=kLoop, calls=%fused_computation.7.clone.1 | loop fusion | flops 4718592 | bytes 38535168 | tf_op jit(solution)/shard_map/while/body/eval_jaxpr/mul | solution.py:107
  447.2 7.1 %pad_maximum_fusion.3 = f32[1536,25,128]{2,0,1:T(8,128)} fusion(f32[1536,24,128]{2,0,1:T(8,128)S(1)} %slice_multiply_fusion.5, f32[1536,1,128]{2,0,1:T(8,128)S(1)} %get-tuple-element.390), kind=kLoop, calls=%fused_computation.6.clone.1 | loop fusion | flops 4915200 | bytes 39321600 | tf_op jit(solution)/shard_map/while/body/eval_jaxpr/concatenate | solution.py:107
  454.3 20.9 %copy.126 = f32[1536,25,25]{1,2,0:T(8,128)} copy(f32[1536,25,25]{0,2,1:T(8,128)} %get-tuple-element.385) | data formatting | bytes 7680000 | tf_op jit(solution)/shard_map/while/body/eval_jaxpr/dot_general | solution.py:93
  475.2 40.7 %fusion.72 = f32[1536,25,128]{2,1,0:T(8,128)S(1)} fusion(f32[1536,25,25]{1,2,0:T(8,128)} %copy.126, f32[1536,25,128]{2,0,1:T(8,128)} %pad_maximum_fusion.3), kind=kOutput, calls=%fused_computation.2.clone.1 | convolution fusion | flops 1474560000 | bytes 43161600 | tf_op jit(solution)/shard_map/while/body/eval_jaxpr/rqp,rqc->rpc/dot_general | solution.py:108
  515.9 4.1 multiply_reduce_fusion.2
  520.1 2.9 select_add_fusion.2
  523.0 2.6 copy_divide_fusion
  (155 shorter events, 50.7 us)
Async XLA Ops:
  6.5 20.6 %copy-start.13 = (bf16[2,2,384,384]{3,2,1,0:T(8,128)(2,1)S(1)}, bf16[2,2,384,384]{3,2,1,0:T(8,128)(2,1)}, u32[]{:S(2)}) copy-start(bf16[2,2,384,384]{3,2,1,0:T(8,128)(2,1)} %param.22) | copy-start | bytes 3538948
  10.7 12.7 %all-to-all-start.4 = ((bf16[16,2,8,128]{3,2,1,0:T(8,128)(2,1)}), bf16[16,2,8,128]{3,2,1,0:T(8,128)(2,1)S(1)}, u32[]{:S(2)}, u32[]{:S(2)}) async-start(bf16[16,2,8,128]{3,2,1,0:T(8,128)(2,1)} %copy.86), calls=%async_computation.4 | async-start | bytes 131072 | tf_op jit(solution)/shard_map/all_to_all | solution.py:35
  19.9 18.5 %copy-start.7 = (bf16[2,640,640]{2,1,0:T(8,128)(2,1)S(1)}, bf16[2,640,640]{2,1,0:T(8,128)(2,1)}, u32[]{:S(2)}) copy-start(bf16[2,640,640]{2,1,0:T(8,128)(2,1)} %param.20) | copy-start | bytes 4915204
  23.4 11.2 %all-to-all-start.3 = ((bf16[16,2,16,256]{3,2,1,0:T(8,128)(2,1)}), bf16[16,2,16,256]{3,2,1,0:T(8,128)(2,1)S(1)}, u32[]{:S(2)}, u32[]{:S(2)}) async-start(bf16[16,2,16,256]{3,2,1,0:T(8,128)(2,1)} %copy.85), calls=%async_computation.3 | async-start | bytes 524288 | tf_op jit(solution)/shard_map/all_to_all | solution.py:35
  34.6 14.0 %all-to-all-start.2 = ((bf16[16,2,24,384]{3,2,1,0:T(8,128)(2,1)}), bf16[16,2,24,384]{3,2,1,0:T(8,128)(2,1)S(1)}, u32[]{:S(2)}, u32[]{:S(2)}) async-start(bf16[16,2,24,384]{3,2,1,0:T(8,128)(2,1)} %copy.84), calls=%async_computation.2 | async-start | bytes 1179648 | tf_op jit(solution)/shard_map/all_to_all | solution.py:35
  48.6 18.1 %all-to-all-start = ((bf16[16,1,40,640]{3,2,1,0:T(8,128)(2,1)}), bf16[16,1,40,640]{3,2,1,0:T(8,128)(2,1)S(1)}, u32[]{:S(2)}, u32[]{:S(2)}) async-start(bf16[16,1,40,640]{3,2,1,0:T(8,128)(2,1)} %bitcast.2), calls=%async_computation | async-start | bytes 1638400 | tf_op jit(solution)/shard_map/all_to_all | solution.py:35
  57.7 30.1 %copy-start.17 = (bf16[64,25,128]{2,0,1:T(8,128)(2,1)S(1)}, bf16[64,25,128]{2,0,1:T(8,128)(2,1)}, u32[]{:S(2)}) copy-start(bf16[64,25,128]{2,0,1:T(8,128)(2,1)} %param.14) | copy-start | bytes 1228804
  66.6 20.3 %all-to-all-start.1 = ((bf16[16,2,32,512]{3,2,1,0:T(8,128)(2,1)}), bf16[16,2,32,512]{3,2,1,0:T(8,128)(2,1)S(1)}, u32[]{:S(2)}, u32[]{:S(2)}) async-start(bf16[16,2,32,512]{3,2,1,0:T(8,128)(2,1)} %copy.83), calls=%async_computation.1 | async-start | bytes 2097152 | tf_op jit(solution)/shard_map/all_to_all | solution.py:35
  71.2 57.0 %all-gather.3.cloned.1.call-start = ((), (), s32[]{:S(2)}) async-start(), calls=%async_computation.5 | async-start | bytes 2959360 | tf_op jit(solution)/shard_map/all_gather | solution.py:47
  87.2 0.7 copy-start.18
  88.2 27.2 %collective-permute-start = (bf16[64,25,128]{2,1,0:T(8,128)(2,1)S(1)}, bf16[64,25,128]{2,1,0:T(8,128)(2,1)S(1)}, u32[]{:S(2)}, u32[]{:S(2)}) collective-permute-start(bf16[64,25,128]{2,1,0:T(8,128)(2,1)S(1)} %copy.80), channel_id=1, source_target_pairs={{0,1},{1,2},{2,3},{3,4},{4,5},{5,6},{6,7},{7,8},{8,9},{9,10},{10,1... | collective-permute-start | bytes 1228808 | tf_op jit(solution)/shard_map/ppermute | solution.py:16
  90.9 37.1 %collective-permute-start.1 = (bf16[64,25,128]{2,1,0:T(8,128)(2,1)S(1)}, bf16[64,25,128]{2,1,0:T(8,128)(2,1)S(1)}, u32[]{:S(2)}, u32[]{:S(2)}) collective-permute-start(bf16[64,25,128]{2,1,0:T(8,128)(2,1)S(1)} %copy.80), channel_id=1, source_target_pairs={{1,0},{2,1},{3,2},{4,3},{5,4},{6,5},{7,6},{8,7},{9,8},{10,9},{11,1... | collective-permute-start | bytes 1228808 | tf_op jit(solution)/shard_map/ppermute | solution.py:17
  131.8 1.0 slice-start
  132.7 4.3 slice-start.1
  133.5 7.2 %slice-start.2 = ((bf16[16,87040]{1,0:T(8,128)(2,1)}), bf16[16,32768]{1,0:T(8,128)(2,1)S(1)}, s32[]{:S(2)}) async-start(bf16[16,87040]{1,0:T(8,128)(2,1)} %reshape.236), calls=%async_computation.8 | async-start | bytes 2097152 | tf_op jit(solution)/shard_map/slice | solution.py:49
  134.6 3.2 copy-start.8
  139.0 1.7 copy-start.4
  141.0 4.1 slice-start.3
  144.1 5.4 %copy-start.19 = (bf16[128,128]{0,1:T(8,128)(2,1)S(1)}, bf16[128,128]{0,1:T(8,128)(2,1)}, u32[]{:S(2)}) copy-start(bf16[128,128]{0,1:T(8,128)(2,1)} %copy.99) | copy-start | bytes 98308
  145.1 3.6 copy-start.9
  145.1 3.6 copy-start.15
  145.1 3.6 copy-start.16
  146.4 3.8 copy-start.14
  146.4 6.1 %copy-start.5 = (bf16[512,512]{0,1:T(8,128)(2,1)S(1)}, bf16[512,512]{0,1:T(8,128)(2,1)}, u32[]{:S(2)}) copy-start(bf16[512,512]{0,1:T(8,128)(2,1)} %neg.17) | copy-start | bytes 1572868
  148.7 3.8 copy-start.6
  150.2 4.0 copy-start.2
  150.2 4.0 copy-start.11
  154.2 6.4 %copy-start.20 = (s32[2]{0:T(128)}, s32[2]{0:T(128)S(1)}, u32[]{:S(2)}) copy-start(s32[2]{0:T(128)S(1)} %get-tuple-element.429) | copy-start | bytes 28 | tf_op jit(solution)/shard_map/while
  154.2 25.2 %copy-start = (bf16[192,25,128]{2,1,0:T(8,128)(2,1)}, bf16[192,25,128]{2,1,0:T(8,128)(2,1)S(1)}, u32[]{:S(2)}) copy-start(bf16[192,25,128]{2,1,0:T(8,128)(2,1)S(1)} %get-tuple-element.432) | copy-start | bytes 3686404 | tf_op jit(solution)/shard_map/while
  249.0 3.9 copy-start.3
  290.9 40.7 %copy-start.10 = (f32[64,48]{1,0:T(8,128)S(1)}, f32[64,48]{1,0:T(8,128)}, u32[]{:S(2)}) copy-start(f32[64,48]{1,0:T(8,128)} %get-tuple-element.439) | copy-start | bytes 36868 | tf_op jit(solution)/shard_map/while
  335.8 2.6 copy-start.1
  335.8 2.6 copy-start.12
  335.8 2.6 copy-start.21
  338.4 6.4 %copy-start.20 = (s32[2]{0:T(128)}, s32[2]{0:T(128)S(1)}, u32[]{:S(2)}) copy-start(s32[2]{0:T(128)S(1)} %get-tuple-element.429) | copy-start | bytes 28 | tf_op jit(solution)/shard_map/while
  338.4 25.2 %copy-start = (bf16[192,25,128]{2,1,0:T(8,128)(2,1)}, bf16[192,25,128]{2,1,0:T(8,128)(2,1)S(1)}, u32[]{:S(2)}) copy-start(bf16[192,25,128]{2,1,0:T(8,128)(2,1)S(1)} %get-tuple-element.432) | copy-start | bytes 3686404 | tf_op jit(solution)/shard_map/while
  433.3 3.9 copy-start.3
  475.2 40.7 %copy-start.10 = (f32[64,48]{1,0:T(8,128)S(1)}, f32[64,48]{1,0:T(8,128)}, u32[]{:S(2)}) copy-start(f32[64,48]{1,0:T(8,128)} %get-tuple-element.439) | copy-start | bytes 36868 | tf_op jit(solution)/shard_map/while
  520.1 2.9 copy-start.1
  520.1 2.9 copy-start.12
  520.1 2.9 copy-start.21
Sparse Core Ops, SparseCore 0:
  88.0 39.1 all-gather.2
where the time goes:
time: 534 us; the launch traced here: 532 us
  local copies, waits for them, and re-layouts  175 us (33%)
  matrix products  172 us (32%)
  other arithmetic  70.9 us (13%)
  waiting for transfers between devices  68.6 us (13%)
  starting transfers between devices  30.9 us (6%)
  between operations  13.7 us (3%)
    dot_general x2, matrix products, messages(): jnp.einsum('rqp,rqc->rpc', dense, gated, precision=lax.Precision.HIGHEST,...  81.3 us
    dot_general x10, matrix products, messages(): output = jnp.dot(inputs, weights[order], preferred_element_type=jnp.float32)  51.5 us
    dot_general x2, local copies, waits for them, and re-layouts, messages(): jnp.dot(frames, table, preferred_element_type=jnp.float32)  41.8 us
    slice x14, local copies, waits for them, and re-layouts, messages(): rotated[:, start:start + width, :].reshape(row_count, width * channels)  40.6 us
    all_to_all x5, waiting for transfers between devices, sum_at_owner(): tiles = lax.all_to_all(cut_along(x, dim, length), axis, 0, 0, tiled=True)  39.8 us
    convert_element_type x2, local copies, waits for them, and re-layouts, messages(): dense_half = dense.astype(jnp.bfloat16)  37.2 us
    dot_general x2, matrix products, messages(): jnp.einsum('rpq,rqc->rpc', dense_half, gathered, preferred_element_type=j...  31.7 us
    all_to_all x5, starting transfers between devices, sum_at_owner(): tiles = lax.all_to_all(cut_along(x, dim, length), axis, 0, 0, tiled=True)  23.8 us
  transfers between devices with their start and end apart: 8, of which 7 were waited for; matrix products, arithmetic and copies ran while one was open for 3% of the time, Pallas kernels for 0%

commit v1 on v0

v1 whole, which is shorter than its diff:
```python
import functools

import jax
import jax.numpy as jnp
import numpy as np
from jax import lax
from jax.experimental import pallas as pl
from jax.experimental.pallas import tpu as pltpu
from jax.sharding import Mesh, PartitionSpec as P

WIDE = ("x", "yl", "core")
NARROW = ("z", "yh")
ATOM_AXES = WIDE + NARROW
SAME_CORE = ("z", "yh", "x", "yl")
C = 128
TILE = 256
WINDOW = 1024
BLOCKS_EACH = 11
FRAME_LANES = 256
INDEX_LANE = 165
DEPTH = (5, 8, 6, 4, 2)
START = (0, 5, 13, 19, 23)
VMEM = 100 * 2**20 // 2


def grouped_place():
    place = {}
    at = 0
    for degree in range(5):
        place[degree * degree + degree] = at
        at += 1
    for order in range(1, 5):
        for sign in (1, -1):
            for degree in range(order, 5):
                place[degree * degree + degree + sign * order] = at
                at += 1
    return place


PLACE = grouped_place()


def block_list():
    blocks = [(0, 0, o, i) for o in range(5) for i in range(5)]
    for order in range(1, 5):
        kept = 5 - order
        blocks += [(order, part, o, i) for part in range(2) for o in range(kept) for i in range(kept)]
    return blocks


BLOCKS = block_list()


def combine_kernel(table, coeff, w0, w1, w2, w3, w4, out, buf, sems):
    arrays = (w0, w1, w2, w3, w4)
    for j in range(BLOCKS_EACH):
        kind = table[j, 0]
        part = table[j, 1]
        row = pl.multiple_of(table[j, 3] * C, C)
        column = pl.multiple_of(table[j, 2] * C, C)
        for a, ref in enumerate(arrays):

            @pl.when(kind == a)
            def _():
                if a == 0:
                    source = ref.at[:, pl.ds(row, C), pl.ds(column, C)]
                else:
                    source = ref.at[:, part, pl.ds(row, C), pl.ds(column, C)]
                pltpu.make_async_copy(source, buf.at[j], sems.at[j]).start()

    for j in range(BLOCKS_EACH):
        pltpu.make_async_copy(w0.at[:, pl.ds(0, C), pl.ds(0, C)], buf.at[j], sems.at[j]).wait()
        total = coeff[0] * buf[j, 0].astype(jnp.float32) + coeff[1] * buf[j, 1].astype(jnp.float32)
        turned = total.T.astype(jnp.bfloat16)
        out[0, 64 * j : 64 * j + 64] = turned[:64]
        out[1, 64 * j : 64 * j + 64] = turned[64:]


def combine(table, coeff, weights):
    return pl.pallas_call(
        combine_kernel,
        grid_spec=pltpu.PrefetchScalarGridSpec(
            num_scalar_prefetch=2,
            grid=(1,),
            in_specs=[pl.BlockSpec(memory_space=pl.ANY)] * 5,
            out_specs=pl.BlockSpec((2, 64 * BLOCKS_EACH, C), lambda i, *_: (0, 0, 0)),
            scratch_shapes=[
                pltpu.VMEM((BLOCKS_EACH, 2, C, C), jnp.bfloat16),
                pltpu.SemaphoreType.DMA((BLOCKS_EACH,)),
            ],
        ),
        out_shape=jax.ShapeDtypeStruct((2, 64 * BLOCKS_EACH, C), jnp.bfloat16),
        compiler_params=pltpu.CompilerParams(vmem_limit_bytes=16 * 2**20),
        cost_estimate=pl.CostEstimate(flops=BLOCKS_EACH * C * C * 4, bytes_accessed=BLOCKS_EACH * C * C * 6, transcendentals=0),
        name="merge_group",
    )(table, coeff, *weights)


def spread_frames(turned, spread):
    for k in range(INDEX_LANE):
        spread[k] = jnp.broadcast_to(turned[k : k + 1, :], (16, TILE)).astype(jnp.bfloat16)


def tree_sum(terms):
    while len(terms) > 1:
        terms = [terms[i] + terms[i + 1] if i + 1 < len(terms) else terms[i] for i in range(0, len(terms), 2)]
    return terms[0]


def rotate_kernel(first, tiles, position, frames, radial, own, low, high, out, out_frames, table, gathered, spread):
    step = pl.program_id(0)

    @pl.when(step == 0)
    def _():
        for q in range(25):
            rows = jnp.concatenate([own[q], low[q], high[q]], axis=0)
            table[q * C : (q + 1) * C, :] = rows.T

    @pl.when(step < tiles[0])
    def _():
        rotate_tile(step, first, position, frames, radial, out, out_frames, table, gathered, spread)


def rotate_tile(step, first, position, frames, radial, out, out_frames, table, gathered, spread):
    begin = first[step]
    edge = lax.broadcasted_iota(jnp.int32, (TILE, C), 0) + step * TILE
    chosen = jnp.concatenate(
        [(position[begin + j] == edge).astype(jnp.float32).astype(jnp.bfloat16) for j in range(WINDOW // C)], axis=1
    )
    window = pl.ds(pl.multiple_of(begin * C, C), WINDOW)
    packed = jnp.dot(chosen, frames[window, :], preferred_element_type=jnp.float32)
    turned = packed.T
    out_frames[0] = turned[:168]
    weights = jnp.dot(chosen, radial[window, :], preferred_element_type=jnp.float32).T
    spread_frames(turned, spread)
    index = turned[INDEX_LANE : INDEX_LANE + 1, :].astype(jnp.int32)
    one_hot = (lax.broadcasted_iota(jnp.int32, (192, TILE), 0) == index).astype(jnp.float32).astype(jnp.bfloat16)
    for q in range(25):
        rows = slice(q * C, (q + 1) * C)
        got = jnp.dot(table[rows, :], one_hot, preferred_element_type=jnp.float32)
        gathered[rows, :] = (got * weights).astype(jnp.bfloat16)

    def channels(chunk, carried):
        at = chunk * 16
        offset = 0
        for degree in range(5):
            size = 2 * degree + 1
            base = degree * degree
            x = [gathered[pl.ds(pl.multiple_of((base + q) * C + at, 16), 16), :] for q in range(size)]
            for p in range(size):
                total = tree_sum([spread[offset + p * size + q] * x[q] for q in range(size)])
                out[0, pl.ds(pl.multiple_of(PLACE[base + p] * C + at, 16), 16), :] = total
            offset += size * size
        return carried

    lax.fori_loop(0, 8, channels, 0)


def rotate(tiles, first, position, frames, radial, own, low, high):
    whole = lambda *shape: pl.BlockSpec(shape, lambda i, *_: (0,) * len(shape))
    most = frames.shape[0] // TILE
    return pl.pallas_call(
        rotate_kernel,
        grid_spec=pltpu.PrefetchScalarGridSpec(
            num_scalar_prefetch=2,
            grid=(most,),
            in_specs=[
                whole(*position.shape),
                whole(*frames.shape),
                whole(*radial.shape),
                whole(*own.shape),
                whole(*own.shape),
                whole(*own.shape),
            ],
            out_specs=[
                pl.BlockSpec((1, 25 * C, TILE), lambda i, f, n: (jnp.minimum(i, n[0] - 1), 0, 0)),
                pl.BlockSpec((1, 168, TILE), lambda i, f, n: (jnp.minimum(i, n[0] - 1), 0, 0)),
            ],
            scratch_shapes=[
                pltpu.VMEM((25 * C, 192), jnp.bfloat16),
                pltpu.VMEM((25 * C, TILE), jnp.bfloat16),
                pltpu.VMEM((INDEX_LANE, 16, TILE), jnp.bfloat16),
            ],
        ),
        out_shape=[
            jax.ShapeDtypeStruct((most, 25 * C, TILE), jnp.bfloat16),
            jax.ShapeDtypeStruct((most, 168, TILE), jnp.float32),
        ],
        compiler_params=pltpu.CompilerParams(vmem_limit_bytes=VMEM),
        cost_estimate=pl.CostEstimate(flops=10**10, bytes_accessed=40 * 10**6, transcendentals=0),
        name="gather_rotate",
    )(first, tiles, position, frames, radial, own, low, high)


def place_weights(core, mine, other, mixes):
    for g, (order, part, o, i) in enumerate(BLOCKS):
        kept = C * DEPTH[order] // 2
        for half, ref in ((core, mine), (1 - core, other)):
            piece = ref[64 * g : 64 * g + 64, :]
            shift = half * 64

            def put(row, column, value):
                mixes[order][pl.ds(pl.multiple_of(row + shift, 64), 64), column : column + C] = value

            if order == 0:
                put(o * C, i * C, piece)
            elif part == 0:
                put(o * C, i * C, piece)
                put(kept + o * C, kept + i * C, piece)
            else:
                put(kept + o * C, i * C, piece)
                put(o * C, kept + i * C, -piece)


def mix_kernel(info, mine, other, rotated, frames, atoms, scale, out, m0, m1, m2, m3, m4, gated, message, spread, total):
    step = pl.program_id(0)
    mixes = (m0, m1, m2, m3, m4)

    @pl.when(step == 0)
    def _():
        place_weights(info[0], mine, other, mixes)
        total[...] = jnp.zeros_like(total)

    @pl.when(step < info[1])
    def _():
        mix_tile(rotated, frames, atoms, mixes, gated, message, spread, total)

    @pl.when(step == pl.num_programs(0) - 1)
    def _():
        for q in range(25):
            out[:, q, :] = total[q] * scale[...]


def mix_tile(rotated, frames, atoms, mixes, gated, message, spread, total):
    first = jnp.dot(mixes[0][...], rotated[0, : 5 * C], preferred_element_type=jnp.float32)
    scalar = first[:C]
    gate = 1.0 / (1.0 + jnp.exp(-scalar))
    for k in range(5):
        gated[k * C : (k + 1) * C] = (first[k * C : (k + 1) * C] * gate).astype(jnp.bfloat16)
    for order in range(1, 5):
        begin = START[order] * C
        size = DEPTH[order]
        mixed = jnp.dot(mixes[order][...], rotated[0, begin : begin + size * C], preferred_element_type=jnp.float32)
        for k in range(size):
            gated[begin + k * C : begin + (k + 1) * C] = (mixed[k * C : (k + 1) * C] * gate).astype(jnp.bfloat16)

    spread_frames(frames[0], spread)

    def channels(chunk, carried):
        at = chunk * 16
        offset = 0
        for degree in range(5):
            size = 2 * degree + 1
            base = degree * degree
            g = [gated[pl.ds(pl.multiple_of(PLACE[base + p] * C + at, 16), 16), :] for p in range(size)]
            for q in range(size):
                value = tree_sum([spread[offset + p * size + q] * g[p] for p in range(size)])
                message[pl.ds(pl.multiple_of((base + q) * C + at, 16), 16), :] = value
            offset += size * size
        return carried

    lax.fori_loop(0, 8, channels, 0)

    owner = (lax.broadcasted_iota(jnp.int32, (64, TILE), 0) == atoms[0]).astype(jnp.float32).astype(jnp.bfloat16)
    for q in range(25):
        total[q] += lax.dot_general(
            owner, message[q * C : (q + 1) * C, :], (((1,), (1,)), ((), ())), preferred_element_type=jnp.float32
        )


def mix(info, mine, other, rotated, frames, atoms, scale):
    whole = lambda *shape: pl.BlockSpec(shape, lambda i, *_: (0,) * len(shape))
    block = lambda a: pl.BlockSpec((1,) + a.shape[1:], lambda i, n: (jnp.minimum(i, n[1] - 1), 0, 0))
    return pl.pallas_call(
        mix_kernel,
        grid_spec=pltpu.PrefetchScalarGridSpec(
            num_scalar_prefetch=1,
            grid=(rotated.shape[0],),
            in_specs=[
                whole(*mine.shape),
                whole(*other.shape),
                block(rotated),
                block(frames),
                block(atoms),
                whole(*scale.shape),
            ],
            out_specs=whole(64, 25, C),
            scratch_shapes=[pltpu.VMEM((d * C, d * C), jnp.bfloat16) for d in DEPTH]
            + [
                pltpu.VMEM((25 * C, TILE), jnp.bfloat16),
                pltpu.VMEM((25 * C, TILE), jnp.bfloat16),
                pltpu.VMEM((INDEX_LANE, 16, TILE), jnp.bfloat16),
                pltpu.VMEM((25, 64, C), jnp.float32),
            ],
        ),
        out_shape=jax.ShapeDtypeStruct((64, 25, C), jnp.float32),
        compiler_params=pltpu.CompilerParams(vmem_limit_bytes=VMEM),
        cost_estimate=pl.CostEstimate(flops=15 * 10**9, bytes_accessed=40 * 10**6, transcendentals=10**6),
        name="mix_messages",
    )(info, mine, other, rotated, frames, atoms, scale)


def body(sizes, node_features, frames, radial, neighbours, counts, coefficients, *weights):
    atoms_here, _, channels = node_features.shape
    slots = neighbours.shape[1]
    edges = atoms_here * slots
    most = edges // TILE
    devices = int(np.prod(list(sizes.values())))
    n_narrow = sizes["z"] * sizes["yh"]
    n_xy = sizes["x"] * sizes["yl"]

    narrow = lax.axis_index(NARROW)
    rows = np.array([BLOCKS[min(g, len(BLOCKS) - 1)] for g in range(n_narrow * BLOCKS_EACH)], np.int32)
    table = lax.dynamic_slice_in_dim(jnp.asarray(rows), narrow * BLOCKS_EACH, BLOCKS_EACH, 0)
    partial = combine(table, coefficients, weights)
    share_rows = partial.shape[1] // n_xy
    parts = lax.all_to_all(partial.reshape(-1, share_rows, C), ("core", "x", "yl"), 0, 0, tiled=True)
    share = jnp.sum(parts.astype(jnp.float32), axis=0).astype(jnp.bfloat16)
    copies = jnp.broadcast_to(share[None], (n_narrow * n_xy,) + share.shape)
    mine = lax.all_to_all(copies, SAME_CORE, 0, 0, tiled=True).reshape(-1, C)
    other = lax.ppermute(mine, "core", [(0, 1), (1, 0)])

    own = node_features.transpose(1, 0, 2)
    up = [(i, (i + 1) % devices) for i in range(devices)]
    low = lax.ppermute(own, ATOM_AXES, up)
    high = lax.ppermute(own, ATOM_AXES, [(b, a) for a, b in up])

    block = lax.axis_index(ATOM_AXES)
    side = (neighbours // atoms_here - block) % devices
    local = neighbours % atoms_here + jnp.where(side == 0, 0, jnp.where(side == 1, 2 * atoms_here, atoms_here))
    before = np.tril(np.ones((atoms_here, atoms_here), np.int32), -1)
    offset = jnp.sum(before * counts[None, :], axis=1)
    ends = offset + counts
    slot = lax.broadcasted_iota(jnp.int32, (atoms_here, slots), 1)
    position = jnp.where(slot < counts[:, None], offset[:, None] + slot, -1).reshape(edges // C, 1, C)
    places = jnp.arange(edges, dtype=jnp.int32)
    atoms = jnp.sum((ends[None, :] <= places[:, None]).astype(jnp.int32), axis=1)
    starts = jnp.arange(most, dtype=jnp.int32) * TILE
    first_atom = jnp.sum((ends[None, :] <= starts[:, None]).astype(jnp.int32), axis=1)
    first = jnp.minimum(first_atom * slots // C, (edges - WINDOW) // C)
    tiles = ((jnp.sum(counts) + TILE - 1) // TILE).astype(jnp.int32).reshape(1)

    filled = jnp.concatenate(
        [
            frames.reshape(edges, -1),
            local.reshape(edges, 1).astype(jnp.bfloat16),
            jnp.zeros((edges, FRAME_LANES - INDEX_LANE - 1), jnp.bfloat16),
        ],
        axis=1,
    )
    rotated, turned = rotate(tiles, first, position, filled, radial.reshape(edges, C), own, low, high)
    scale = jnp.broadcast_to(1.0 / jnp.sqrt(counts.astype(jnp.float32))[:, None], (atoms_here, C))
    info = jnp.concatenate([lax.axis_index("core").astype(jnp.int32).reshape(1), tiles])
    return mix(info, mine, other, rotated, turned, atoms.reshape(most, 1, TILE), scale)


def solution(mesh):
    sizes = {"x": mesh.shape["wide"] // 4, "yl": 2, "core": 2, "z": mesh.shape["narrow"] // 2, "yh": 2}
    fine = Mesh(mesh.devices.reshape(tuple(sizes.values())), tuple(sizes))
    in_specs = (
        P(ATOM_AXES, None, None),
        P(ATOM_AXES, None, None),
        P(ATOM_AXES, None, None),
        P(ATOM_AXES, None),
        P(ATOM_AXES),
        P(WIDE),
        P(WIDE, None, None),
        P(WIDE, None, None, None),
        P(WIDE, None, None, None),
        P(WIDE, None, None, None),
        P(WIDE, None, None, None),
    )
    out_specs = P(ATOM_AXES, None, None)
    return jax.shard_map(functools.partial(body, sizes), mesh=fine, in_specs=in_specs, out_specs=out_specs, check_vma=False)
```

time: 534 us -> 119 us (0.22)
  the two profiles are of different devices: /device:TPU:1 before, /device:TPU:0 now
where the time goes in v1:
time: 119 us; the launch traced here: 118 us
  Pallas kernels  55.6 us (47%)
  waiting for transfers between devices  25.6 us (22%)
  starting transfers between devices  18.9 us (16%)
  local copies, waits for them, and re-layouts  13.6 us (11%)
  other arithmetic  3.58 us (3%)
    pallas_call x1, Pallas kernels, mix(): pl.pallas_call(mix_kernel, grid_spec=pltpu.PrefetchScalarGridSpec(num_sca...  31.2 us
    pallas_call x1, Pallas kernels, rotate(): pl.pallas_call(rotate_kernel, grid_spec=pltpu.PrefetchScalarGridSpec(num_...  21.2 us
    all_to_all x1, waiting for transfers between devices, body(): mine = lax.all_to_all(copies, SAME_CORE, 0, 0, tiled=True).reshape(-1, C)  17.9 us
    unnamed x22, local copies, waits for them, and re-layouts  8.04 us
    all_to_all x1, waiting for transfers between devices, body(): lax.all_to_all(partial.reshape(-1, share_rows, C), ('core', 'x', 'yl'), 0...  7.72 us
    all_to_all x1, starting transfers between devices, body(): mine = lax.all_to_all(copies, SAME_CORE, 0, 0, tiled=True).reshape(-1, C)  7.12 us
    ppermute x1, starting transfers between devices, body(): high = lax.ppermute(own, ATOM_AXES, [(b, a) for a, b in up])  4.93 us
    all_to_all x1, starting transfers between devices, body(): lax.all_to_all(partial.reshape(-1, share_rows, C), ('core', 'x', 'yl'), 0...  3.56 us
  transfers between devices with their start and end apart: 5, of which 2 were waited for; matrix products, arithmetic and copies ran while one was open for 7% of the time, Pallas kernels for 21%

profile of v1, /device:TPU:0, one launch (start us, length us, event | category | flops | bytes accessed | tf_op | source)
XLA Modules:
  0.0 118.0 jit_solution(10767435703486491038)
XLA Ops:
  0.0 3.3 %collective-permute-start.1 = (bf16[25,64,128]{2,1,0:T(8,128)(2,1)}, bf16[25,64,128]{2,1,0:T(8,128)(2,1)}, u32[]{:S(2)}, u32[]{:S(2)}) collective-permute-start(bf16[25,64,128]{2,1,0:T(8,128)(2,1)} %bitcast.14), channel_id=1, source_target_pairs={{0,1},{1,2},{2,3},{3,4},{4,5},{5,6},{6,7},{7,8},{8,9},{9,10},{10,1... | collective-permute-start | bytes 1228808 | tf_op jit(solution)/shard_map/ppermute | solution.py:325
  3.3 4.9 %collective-permute-start.2 = (bf16[25,64,128]{2,1,0:T(8,128)(2,1)}, bf16[25,64,128]{2,1,0:T(8,128)(2,1)}, u32[]{:S(2)}, u32[]{:S(2)}) collective-permute-start(bf16[25,64,128]{2,1,0:T(8,128)(2,1)} %bitcast.15), channel_id=1, source_target_pairs={{1,0},{2,1},{3,2},{4,3},{5,4},{6,5},{7,6},{8,7},{9,8},{10,9},{11,1... | collective-permute-start | bytes 1228808 | tf_op jit(solution)/shard_map/ppermute | solution.py:326
  8.2 0.7 constant_dynamic-slice_fusion.table
  8.9 0.0 copy-start
  8.9 1.6 %copy-done = bf16[2,2,512,512]{3,2,1,0:T(8,128)(2,1)S(1)} copy-done((bf16[2,2,512,512]{3,2,1,0:T(8,128)(2,1)S(1)}, bf16[2,2,512,512]{3,2,1,0:T(8,128)(2,1)}, u32[]{:S(2)}) %copy-start) | copy-done | bytes 2097176
  10.5 0.0 copy-start.1
  10.5 1.4 %copy-done.1 = bf16[2,640,640]{2,1,0:T(8,128)(2,1)S(1)} copy-done((bf16[2,640,640]{2,1,0:T(8,128)(2,1)S(1)}, bf16[2,640,640]{2,1,0:T(8,128)(2,1)}, u32[]{:S(2)}) %copy-start.1) | copy-done | bytes 1638424
  11.9 0.0 copy-start.2
  11.9 1.3 %copy-done.2 = bf16[2,2,384,384]{3,2,1,0:T(8,128)(2,1)S(1)} copy-done((bf16[2,2,384,384]{3,2,1,0:T(8,128)(2,1)S(1)}, bf16[2,2,384,384]{3,2,1,0:T(8,128)(2,1)}, u32[]{:S(2)}) %copy-start.2) | copy-done | bytes 1179672
  13.2 0.0 copy-start.3
  13.2 1.0 copy-done.3
  14.3 0.0 copy-start.4
  14.3 0.9 copy-done.4
  15.2 0.0 copy-start.5
  15.2 0.7 copy-done.5
  15.8 0.0 copy-start.8
  15.8 0.0 copy-start.10
  15.8 3.1 %merge_group.1 = bf16[2,704,128]{2,1,0:T(8,128)(2,1)} custom-call(s32[11,4]{1,0:T(8,128)S(1)} %constant_dynamic-slice_fusion.table, f32[2]{0:T(128)S(1)} %copy-done.5, bf16[2,640,640]{2,1,0:T(8,128)(2,1)S(1)} %copy-done.1, bf16[2,2,512,512]{3,2,1,0:T(8,128)(2,1)S(1)} %copy-done, bf16[2,2,384,384]{3,2,1,0:T(8,128)(2,1)S(1)} %copy-done.2, ...), custom_call_target="tpu_custom_call" | custom-call | flops 720896 | bytes 1081344 | tf_op jit(solution)/shard_map/merge_group/pallas_call | solution.py:80
  19.0 3.6 %all-to-all-start = ((bf16[16,88,128]{2,1,0:T(8,128)(2,1)}), bf16[16,88,128]{2,1,0:T(8,128)(2,1)S(1)}, u32[]{:S(2)}, u32[]{:S(2)}) async-start(bf16[16,88,128]{2,1,0:T(8,128)(2,1)} %bitcast.2), calls=%async_computation | async-start | bytes 720896 | tf_op jit(solution)/shard_map/all_to_all | solution.py:317
  22.5 0.0 copy-done.8
  22.5 0.0 copy-done.10
  22.5 0.1 multiply_reduce_fusion
  22.7 0.6 fusion.7
  23.9 7.7 %all-to-all-done = bf16[16,88,128]{2,1,0:T(8,128)(2,1)S(1)} async-done(((bf16[16,88,128]{2,1,0:T(8,128)(2,1)}), bf16[16,88,128]{2,1,0:T(8,128)(2,1)S(1)}, u32[]{:S(2)}, u32[]{:S(2)}) %all-to-all-start) | async-done | bytes 360480 | tf_op jit(solution)/shard_map/all_to_all | solution.py:317
  31.6 0.1 reduce_sum.49
  31.7 1.3 %broadcast_in_dim.16 = bf16[64,88,128]{2,1,0:T(8,128)(2,1)} broadcast(bf16[88,128]{1,0:T(8,128)(2,1)S(1)} %reduce_sum.49), dimensions={1,2} | broadcast | bytes 1464320 | tf_op jit(solution)/shard_map/broadcast_in_dim | solution.py:319
  33.0 0.0 copy-start.9
  33.0 7.1 %all-to-all-start.1 = ((bf16[64,88,128]{2,1,0:T(8,128)(2,1)}), bf16[64,88,128]{2,1,0:T(8,128)(2,1)S(1)}, u32[]{:S(2)}, u32[]{:S(2)}) async-start(bf16[64,88,128]{2,1,0:T(8,128)(2,1)} %broadcast_in_dim.16), calls=%async_computation.1 | async-start | bytes 2883584 | tf_op jit(solution)/shard_map/all_to_all | solution.py:320
  40.1 0.0 copy-done.9
  40.2 0.1 copy.23
  40.3 1.8 %convert_element_type.30 = bf16[3072,1]{1,0:T(8,128)(2,1)} reshape(bf16[64,48]{1,0:T(8,128)(2,1)S(1)} %copy.23) | data formatting | bytes 12288 | tf_op jit(solution)/shard_map/convert_element_type | solution.py:346
  42.0 0.1 copy.22
  42.1 0.1 select_n.54
  42.2 0.1 pad.2.clone
  42.3 0.2 convert_reduce_fusion.1
  42.5 0.2 convert_reduce_fusion
  42.6 0.0 copy-start.7
  42.6 2.3 %maximum_maximum_fusion.frames = bf16[3072,256]{1,0:T(8,128)(2,1)S(1)} fusion(bf16[3072,1]{1,0:T(8,128)(2,1)} %convert_element_type.30, bf16[3072,165]{1,0:T(8,128)(2,1)} %bitcast.17, bf16[256]{0:T(256)(128)(2,1)S(1)} %pad.2.clone), kind=kLoop, calls=%fused_computation | loop fusion | flops 4718592 | bytes 2593280 | tf_op jit(solution)/shard_map/concatenate | solution.py:343
  44.9 17.9 %all-to-all-done.1 = bf16[64,88,128]{2,1,0:T(8,128)(2,1)S(1)} async-done(((bf16[64,88,128]{2,1,0:T(8,128)(2,1)}), bf16[64,88,128]{2,1,0:T(8,128)(2,1)S(1)}, u32[]{:S(2)}, u32[]{:S(2)}) %all-to-all-start.1) | async-done | bytes 1441824 | tf_op jit(solution)/shard_map/all_to_all | solution.py:320
  62.8 0.0 collective-permute-start
  62.8 0.1 pad_add_fusion.info
  62.9 0.0 collective-permute-done.1.low
  62.9 0.0 collective-permute-done.2.high
  62.9 0.0 copy-done.7
  62.9 0.0 copy-start.6
  62.9 1.1 copy-done.6
  64.1 21.2 %gather_rotate.1 = (bf16[12,3200,256]{2,1,0:T(8,128)(2,1)}, f32[12,168,256]{2,1,0:T(8,128)}) custom-call(s32[12]{0:T(128)S(1)} %fusion.6.first, s32[1]{0:T(128)} %bitcast.1.tiles, s32[24,1,128]{2,1,0:T(1,128)S(1)} %bitcast.12, bf16[3072,256]{1,0:T(8,128)(2,1)S(1)} %maximum_maximum_fusion.frames, bf16[3072,128]{1,0:T(8,128)(2,1)S(1)} %bitcast.13, ...), custom_call_target="tpu_custom_call" | custom-call | flops 10000000000 | bytes 40000000 | tf_op jit(solution)/shard_map/gather_rotate/pallas_call | solution.py:162
  85.3 0.0 collective-permute-done.other
  85.3 0.1 broadcast_in_dim.19.scale
  85.4 31.2 %mix_messages.1 = f32[64,25,128]{2,1,0:T(8,128)S(1)} custom-call(s32[2]{0:T(128)S(1)} %pad_add_fusion.info, bf16[5632,128]{1,0:T(8,128)(2,1)S(1)} %bitcast.10, bf16[5632,128]{1,0:T(8,128)(2,1)S(1)} %collective-permute-done.other, bf16[12,3200,256]{2,1,0:T(8,128)(2,1)} %get-tuple-element.7.rotated, f32[12,168,256]{2,1,0:T(8,128)} %get-tuple-element.8.frames, ...), custom_call_target="tpu_custom_call" | custom-call | flops 15000000512 | bytes 40000000 | tf_op jit(solution)/shard_map/mix_messages/pallas_call | solution.py:274
  116.6 1.4 %copy.26 = f32[64,25,128]{2,0,1:T(8,128)} copy(f32[64,25,128]{2,1,0:T(8,128)S(1)} %mix_messages.1) | data formatting | bytes 1638400 | tf_op jit(solution)/shard_map/mix_messages/pallas_call | solution.py:274
  (6 shorter events, 0.1 us)
Async XLA Ops:
  0.0 62.9 %collective-permute-start.1 = (bf16[25,64,128]{2,1,0:T(8,128)(2,1)}, bf16[25,64,128]{2,1,0:T(8,128)(2,1)}, u32[]{:S(2)}, u32[]{:S(2)}) collective-permute-start(bf16[25,64,128]{2,1,0:T(8,128)(2,1)} %bitcast.14), channel_id=1, source_target_pairs={{0,1},{1,2},{2,3},{3,4},{4,5},{5,6},{6,7},{7,8},{8,9},{9,10},{10,1... | collective-permute-start | bytes 1228808 | tf_op jit(solution)/shard_map/ppermute | solution.py:325
  3.3 59.6 %collective-permute-start.2 = (bf16[25,64,128]{2,1,0:T(8,128)(2,1)}, bf16[25,64,128]{2,1,0:T(8,128)(2,1)}, u32[]{:S(2)}, u32[]{:S(2)}) collective-permute-start(bf16[25,64,128]{2,1,0:T(8,128)(2,1)} %bitcast.15), channel_id=1, source_target_pairs={{1,0},{2,1},{3,2},{4,3},{5,4},{6,5},{7,6},{8,7},{9,8},{10,9},{11,1... | collective-permute-start | bytes 1228808 | tf_op jit(solution)/shard_map/ppermute | solution.py:326
  8.9 1.6 %copy-start = (bf16[2,2,512,512]{3,2,1,0:T(8,128)(2,1)S(1)}, bf16[2,2,512,512]{3,2,1,0:T(8,128)(2,1)}, u32[]{:S(2)}) copy-start(bf16[2,2,512,512]{3,2,1,0:T(8,128)(2,1)} %w1.1) | copy-start | bytes 6291460
  10.5 1.4 %copy-start.1 = (bf16[2,640,640]{2,1,0:T(8,128)(2,1)S(1)}, bf16[2,640,640]{2,1,0:T(8,128)(2,1)}, u32[]{:S(2)}) copy-start(bf16[2,640,640]{2,1,0:T(8,128)(2,1)} %w0.1) | copy-start | bytes 4915204
  11.9 1.3 %copy-start.2 = (bf16[2,2,384,384]{3,2,1,0:T(8,128)(2,1)S(1)}, bf16[2,2,384,384]{3,2,1,0:T(8,128)(2,1)}, u32[]{:S(2)}) copy-start(bf16[2,2,384,384]{3,2,1,0:T(8,128)(2,1)} %w2.1) | copy-start | bytes 3538948
  13.2 1.0 copy-start.3
  14.3 0.9 copy-start.4
  15.2 0.7 copy-start.5
  15.8 6.7 %copy-start.8 = (s32[64,64]{1,0:T(8,128)S(1)}, s32[64,64]{1,0:T(8,128)}, u32[]{:S(2)}) copy-start(s32[64,64]{1,0:T(8,128)} %constant.115.clone) | copy-start | bytes 49156
  15.8 6.7 %copy-start.10 = (s32[64]{0:T(128)S(1)}, s32[64]{0:T(128)}, u32[]{:S(2)}) copy-start(s32[64]{0:T(128)} %param.17) | copy-start | bytes 772
  19.0 12.6 %all-to-all-start = ((bf16[16,88,128]{2,1,0:T(8,128)(2,1)}), bf16[16,88,128]{2,1,0:T(8,128)(2,1)S(1)}, u32[]{:S(2)}, u32[]{:S(2)}) async-start(bf16[16,88,128]{2,1,0:T(8,128)(2,1)} %bitcast.2), calls=%async_computation | async-start | bytes 720896 | tf_op jit(solution)/shard_map/all_to_all | solution.py:317
  33.0 7.1 %copy-start.9 = (s32[64,48]{0,1:T(8,128)S(1)}, s32[64,48]{0,1:T(8,128)}, u32[]{:S(2)}) copy-start(s32[64,48]{0,1:T(8,128)} %param.16) | copy-start | bytes 36868
  33.0 29.8 %all-to-all-start.1 = ((bf16[64,88,128]{2,1,0:T(8,128)(2,1)}), bf16[64,88,128]{2,1,0:T(8,128)(2,1)S(1)}, u32[]{:S(2)}, u32[]{:S(2)}) async-start(bf16[64,88,128]{2,1,0:T(8,128)(2,1)} %broadcast_in_dim.16), calls=%async_computation.1 | async-start | bytes 2883584 | tf_op jit(solution)/shard_map/all_to_all | solution.py:320
  42.6 20.3 %copy-start.7 = (bf16[64,25,128]{2,0,1:T(8,128)(2,1)S(1)}, bf16[64,25,128]{2,0,1:T(8,128)(2,1)}, u32[]{:S(2)}) copy-start(bf16[64,25,128]{2,0,1:T(8,128)(2,1)} %param.13) | copy-start | bytes 1228804
  62.8 22.5 %collective-permute-start = (bf16[5632,128]{1,0:T(8,128)(2,1)S(1)}, bf16[5632,128]{1,0:T(8,128)(2,1)S(1)}, u32[]{:S(2)}, u32[]{:S(2)}) collective-permute-start(bf16[5632,128]{1,0:T(8,128)(2,1)S(1)} %bitcast.9), channel_id=1, source_target_pairs={{0,8},{8,0},{1,9},{9,1},{2,10},{10,2},{3,11},{11,3},{4,12},{12,4},... | collective-permute-start | bytes 4325384 | tf_op jit(solution)/shard_map/ppermute | solution.py:321
  62.9 1.1 copy-start.6

commit v2 on v1

--- a/solution.py
+++ b/solution.py
@@ -16,7 +16,6 @@
 TILE = 256
 WINDOW = 1024
 BLOCKS_EACH = 11
-FRAME_LANES = 256
 INDEX_LANE = 165
 DEPTH = (5, 8, 6, 4, 2)
 START = (0, 5, 13, 19, 23)
@@ -82,7 +81,7 @@
         grid_spec=pltpu.PrefetchScalarGridSpec(
             num_scalar_prefetch=2,
             grid=(1,),
-            in_specs=[pl.BlockSpec(memory_space=pl.ANY)] * 5,
+            in_specs=[pl.BlockSpec(memory_space=pltpu.HBM)] * 5,
             out_specs=pl.BlockSpec((2, 64 * BLOCKS_EACH, C), lambda i, *_: (0, 0, 0)),
             scratch_shapes=[
                 pltpu.VMEM((BLOCKS_EACH, 2, C, C), jnp.bfloat16),
@@ -90,7 +89,7 @@
             ],
         ),
         out_shape=jax.ShapeDtypeStruct((2, 64 * BLOCKS_EACH, C), jnp.bfloat16),
-        compiler_params=pltpu.CompilerParams(vmem_limit_bytes=16 * 2**20),
+        compiler_params=pltpu.CompilerParams(vmem_limit_bytes=62 * 2**20),
         cost_estimate=pl.CostEstimate(flops=BLOCKS_EACH * C * C * 4, bytes_accessed=BLOCKS_EACH * C * C * 6, transcendentals=0),
         name="merge_group",
     )(table, coeff, *weights)
@@ -107,7 +106,49 @@
     return terms[0]
 
 
-def rotate_kernel(first, tiles, position, frames, radial, own, low, high, out, out_frames, table, gathered, spread):
+def compact_kernel(first, tiles, position, local, frames, radial, out_frames, out_radial):
+    step = pl.program_id(0)
+
+    @pl.when(step < tiles[0])
+    def _():
+        begin = first[step]
+        edge = lax.broadcasted_iota(jnp.int32, (TILE, C), 0) + step * TILE
+        chosen = jnp.concatenate(
+            [(position[begin + j] == edge).astype(jnp.float32).astype(jnp.bfloat16) for j in range(WINDOW // C)], axis=1
+        )
+        window = pl.ds(pl.multiple_of(begin * C, C), WINDOW)
+        packed = jnp.dot(chosen, frames[window, :], preferred_element_type=jnp.float32)
+        out_frames[0, :INDEX_LANE] = packed.T
+        index = jnp.concatenate([local[begin + j] for j in range(WINDOW // C)], axis=1)
+        index = jnp.broadcast_to(index, (8, WINDOW)).astype(jnp.bfloat16)
+        moved = lax.dot_general(index, chosen, (((1,), (1,)), ((), ())), preferred_element_type=jnp.float32)
+        out_frames[0, INDEX_LANE : INDEX_LANE + 1] = moved[:1]
+        out_radial[0] = jnp.dot(chosen, radial[window, :], preferred_element_type=jnp.float32).T
+
+
+def compact(tiles, first, position, local, frames, radial):
+    whole = lambda *shape: pl.BlockSpec(shape, lambda i, *_: (0,) * len(shape))
+    most = frames.shape[0] // TILE
+    tile = lambda rows: pl.BlockSpec((1, rows, TILE), lambda i, f, n: (jnp.minimum(i, n[0] - 1), 0, 0))
+    return pl.pallas_call(
+        compact_kernel,
+        grid_spec=pltpu.PrefetchScalarGridSpec(
+            num_scalar_prefetch=2,
+            grid=(most,),
+            in_specs=[whole(*a.shape) for a in (position, local, frames, radial)],
+            out_specs=[tile(168), tile(C)],
+        ),
+        out_shape=[
+            jax.ShapeDtypeStruct((most, 168, TILE), jnp.float32),
+            jax.ShapeDtypeStruct((most, C, TILE), jnp.float32),
+        ],
+        compiler_params=pltpu.CompilerParams(vmem_limit_bytes=VMEM),
+        cost_estimate=pl.CostEstimate(flops=2 * 10**10, bytes_accessed=40 * 10**6, transcendentals=0),
+        name="compact_edges",
+    )(first, tiles, position, local, frames, radial)
+
+
+def rotate_kernel(tiles, frames, radial, own, low, high, out, table, gathered, spread):
     step = pl.program_id(0)
 
     @pl.when(step == 0)
@@ -118,27 +159,17 @@
 
     @pl.when(step < tiles[0])
     def _():
-        rotate_tile(step, first, position, frames, radial, out, out_frames, table, gathered, spread)
-
-
-def rotate_tile(step, first, position, frames, radial, out, out_frames, table, gathered, spread):
-    begin = first[step]
-    edge = lax.broadcasted_iota(jnp.int32, (TILE, C), 0) + step * TILE
-    chosen = jnp.concatenate(
-        [(position[begin + j] == edge).astype(jnp.float32).astype(jnp.bfloat16) for j in range(WINDOW // C)], axis=1
-    )
-    window = pl.ds(pl.multiple_of(begin * C, C), WINDOW)
-    packed = jnp.dot(chosen, frames[window, :], preferred_element_type=jnp.float32)
-    turned = packed.T
-    out_frames[0] = turned[:168]
-    weights = jnp.dot(chosen, radial[window, :], preferred_element_type=jnp.float32).T
-    spread_frames(turned, spread)
-    index = turned[INDEX_LANE : INDEX_LANE + 1, :].astype(jnp.int32)
+        rotate_tile(frames, radial, out, table, gathered, spread)
+
+
+def rotate_tile(frames, radial, out, table, gathered, spread):
+    spread_frames(frames[0], spread)
+    index = frames[0, INDEX_LANE : INDEX_LANE + 1, :].astype(jnp.int32)
     one_hot = (lax.broadcasted_iota(jnp.int32, (192, TILE), 0) == index).astype(jnp.float32).astype(jnp.bfloat16)
     for q in range(25):
         rows = slice(q * C, (q + 1) * C)
         got = jnp.dot(table[rows, :], one_hot, preferred_element_type=jnp.float32)
-        gathered[rows, :] = (got * weights).astype(jnp.bfloat16)
+        gathered[rows, :] = (got * radial[0]).astype(jnp.bfloat16)
 
     def channels(chunk, carried):
         at = chunk * 16
@@ -156,40 +187,28 @@
     lax.fori_loop(0, 8, channels, 0)
 
 
-def rotate(tiles, first, position, frames, radial, own, low, high):
+def rotate(tiles, frames, radial, own, low, high):
     whole = lambda *shape: pl.BlockSpec(shape, lambda i, *_: (0,) * len(shape))
-    most = frames.shape[0] // TILE
+    most = frames.shape[0]
+    tile = lambda rows: pl.BlockSpec((1, rows, TILE), lambda i, n: (jnp.minimum(i, n[0] - 1), 0, 0))
     return pl.pallas_call(
         rotate_kernel,
         grid_spec=pltpu.PrefetchScalarGridSpec(
-            num_scalar_prefetch=2,
+            num_scalar_prefetch=1,
             grid=(most,),
-            in_specs=[
-                whole(*position.shape),
-                whole(*frames.shape),
-                whole(*radial.shape),
-                whole(*own.shape),
-                whole(*own.shape),
-                whole(*own.shape),
-            ],
-            out_specs=[
-                pl.BlockSpec((1, 25 * C, TILE), lambda i, f, n: (jnp.minimum(i, n[0] - 1), 0, 0)),
-                pl.BlockSpec((1, 168, TILE), lambda i, f, n: (jnp.minimum(i, n[0] - 1), 0, 0)),
-            ],
+            in_specs=[tile(168), tile(C)] + [whole(*own.shape)] * 3,
+            out_specs=tile(25 * C),
             scratch_shapes=[
                 pltpu.VMEM((25 * C, 192), jnp.bfloat16),
                 pltpu.VMEM((25 * C, TILE), jnp.bfloat16),
                 pltpu.VMEM((INDEX_LANE, 16, TILE), jnp.bfloat16),
             ],
         ),
-        out_shape=[
-            jax.ShapeDtypeStruct((most, 25 * C, TILE), jnp.bfloat16),
-            jax.ShapeDtypeStruct((most, 168, TILE), jnp.float32),
-        ],
+        out_shape=jax.ShapeDtypeStruct((most, 25 * C, TILE), jnp.bfloat16),
         compiler_params=pltpu.CompilerParams(vmem_limit_bytes=VMEM),
         cost_estimate=pl.CostEstimate(flops=10**10, bytes_accessed=40 * 10**6, transcendentals=0),
         name="gather_rotate",
-    )(first, tiles, position, frames, radial, own, low, high)
+    )(tiles, frames, radial, own, low, high)
 
 
 def place_weights(core, mine, other, mixes):
@@ -228,7 +247,7 @@
     @pl.when(step == pl.num_programs(0) - 1)
     def _():
         for q in range(25):
-            out[:, q, :] = total[q] * scale[...]
+            out[q] = total[q] * scale[...]
 
 
 def mix_tile(rotated, frames, atoms, mixes, gated, message, spread, total):
@@ -284,7 +303,7 @@
                 block(atoms),
                 whole(*scale.shape),
             ],
-            out_specs=whole(64, 25, C),
+            out_specs=whole(25, 64, C),
             scratch_shapes=[pltpu.VMEM((d * C, d * C), jnp.bfloat16) for d in DEPTH]
             + [
                 pltpu.VMEM((25 * C, TILE), jnp.bfloat16),
@@ -293,7 +312,7 @@
                 pltpu.VMEM((25, 64, C), jnp.float32),
             ],
         ),
-        out_shape=jax.ShapeDtypeStruct((64, 25, C), jnp.float32),
+        out_shape=jax.ShapeDtypeStruct((25, 64, C), jnp.float32),
         compiler_params=pltpu.CompilerParams(vmem_limit_bytes=VMEM),
         cost_estimate=pl.CostEstimate(flops=15 * 10**9, bytes_accessed=40 * 10**6, transcendentals=10**6),
         name="mix_messages",
@@ -318,12 +337,6 @@
     share = jnp.sum(parts.astype(jnp.float32), axis=0).astype(jnp.bfloat16)
     copies = jnp.broadcast_to(share[None], (n_narrow * n_xy,) + share.shape)
     mine = lax.all_to_all(copies, SAME_CORE, 0, 0, tiled=True).reshape(-1, C)
-    other = lax.ppermute(mine, "core", [(0, 1), (1, 0)])
-
-    own = node_features.transpose(1, 0, 2)
-    up = [(i, (i + 1) % devices) for i in range(devices)]
-    low = lax.ppermute(own, ATOM_AXES, up)
-    high = lax.ppermute(own, ATOM_AXES, [(b, a) for a, b in up])
 
     block = lax.axis_index(ATOM_AXES)
     side = (neighbours // atoms_here - block) % devices
@@ -340,18 +353,21 @@
     first = jnp.minimum(first_atom * slots // C, (edges - WINDOW) // C)
     tiles = ((jnp.sum(counts) + TILE - 1) // TILE).astype(jnp.int32).reshape(1)
 
-    filled = jnp.concatenate(
-        [
-            frames.reshape(edges, -1),
-            local.reshape(edges, 1).astype(jnp.bfloat16),
-            jnp.zeros((edges, FRAME_LANES - INDEX_LANE - 1), jnp.bfloat16),
-        ],
-        axis=1,
+    own, first, position, _ = lax.optimization_barrier((node_features.transpose(1, 0, 2), first, position, partial))
+    turned, factor = compact(
+        tiles, first, position, local.reshape(position.shape), frames.reshape(edges, -1), radial.reshape(edges, C)
     )
-    rotated, turned = rotate(tiles, first, position, filled, radial.reshape(edges, C), own, low, high)
+    up = [(i, (i + 1) % devices) for i in range(devices)]
+    low = lax.ppermute(own, ATOM_AXES, up)
+    high = lax.ppermute(own, ATOM_AXES, [(b, a) for a, b in up])
+    turned, low, high = lax.optimization_barrier((turned, low, high))
+    rotated = rotate(tiles, turned, factor, own, low, high)
+    mine, rotated, turned = lax.optimization_barrier((mine, rotated, turned))
+    other = lax.ppermute(mine, "core", [(0, 1), (1, 0)])
     scale = jnp.broadcast_to(1.0 / jnp.sqrt(counts.astype(jnp.float32))[:, None], (atoms_here, C))
     info = jnp.concatenate([lax.axis_index("core").astype(jnp.int32).reshape(1), tiles])
-    return mix(info, mine, other, rotated, turned, atoms.reshape(most, 1, TILE), scale)
+    out = mix(info, mine, other, rotated, turned, atoms.reshape(most, 1, TILE), scale)
+    return out.transpose(1, 0, 2)
 
 
 def solution(mesh):

time: 119 us -> 104 us (0.87)
  the two profiles are of different devices: /device:TPU:0 before, /device:TPU:56 now
where the time goes in v2:
time: 104 us; the launch traced here: 103 us
  Pallas kernels  59 us (57%)
  starting transfers between devices  19.4 us (19%)
  waiting for transfers between devices  18.5 us (18%)
  local copies, waits for them, and re-layouts  4.13 us (4%)
  other arithmetic  1.3 us (1%)
    pallas_call x1, Pallas kernels, mix(): pl.pallas_call(mix_kernel, grid_spec=pltpu.PrefetchScalarGridSpec(num_sca...  31.4 us
    pallas_call x1, Pallas kernels, rotate(): pl.pallas_call(rotate_kernel, grid_spec=pltpu.PrefetchScalarGridSpec(num_...  16.7 us
    ppermute x1, waiting for transfers between devices, body(): high = lax.ppermute(own, ATOM_AXES, [(b, a) for a, b in up])  13.3 us
    all_to_all x1, starting transfers between devices, body(): mine = lax.all_to_all(copies, SAME_CORE, 0, 0, tiled=True).reshape(-1, C)  10 us
    pallas_call x1, Pallas kernels, compact(): pl.pallas_call(compact_kernel, grid_spec=pltpu.PrefetchScalarGridSpec(num...  7.11 us
    all_to_all x1, starting transfers between devices, body(): lax.all_to_all(partial.reshape(-1, share_rows, C), ('core', 'x', 'yl'), 0...  5.79 us
    pallas_call x1, Pallas kernels, combine(): pl.pallas_call(combine_kernel, grid_spec=pltpu.PrefetchScalarGridSpec(num...  3.81 us
    ppermute x1, waiting for transfers between devices, body(): other = lax.ppermute(mine, 'core', [(0, 1), (1, 0)])  2.96 us
  transfers between devices with their start and end apart: 5, of which 3 were waited for; matrix products, arithmetic and copies ran while one was open for 3% of the time, Pallas kernels for 23%

profile of v2, /device:TPU:56, one launch (start us, length us, event | category | flops | bytes accessed | tf_op | source)
XLA Modules:
  0.0 103.0 jit_solution(2693065879211184033)
XLA Ops:
  0.0 1.3 %constant_dynamic-slice_fusion.table = s32[11,4]{1,0:T(8,128)} fusion(s32[88,4]{1,0:T(8,128)} %constant.113.clone, s32[]{:T(128)S(6)} %select_n.51), kind=kLoop, calls=%fused_computation.28 | loop fusion | bytes 356 | tf_op jit(solution)/shard_map/dynamic_slice | solution.py:333
  1.3 0.0 copy-start.3
  1.3 0.0 copy-start.5
  1.3 0.0 copy-start.2
  1.3 0.0 copy-start.4
  1.3 3.8 %merge_group.1 = bf16[2,704,128]{2,1,0:T(8,128)(2,1)} custom-call(s32[11,4]{1,0:T(8,128)} %constant_dynamic-slice_fusion.table, f32[2]{0:T(128)} %coeff.1, bf16[2,640,640]{2,1,0:T(8,128)(2,1)} %w0.1, bf16[2,2,512,512]{3,2,1,0:T(8,128)(2,1)} %w1.1, bf16[2,2,384,384]{3,2,1,0:T(8,128)(2,1)} %w2.1, bf16[2,2,256,256]{3,2,1,0:T(8,128)(2,1)} %w3.1, ...), custom_call_target="tpu_custom_call" | custom-call | flops 720896 | bytes 1081344 | tf_op jit(solution)/shard_map/merge_group/pallas_call | solution.py:79
  5.1 5.8 %all-to-all-start = ((bf16[16,88,128]{2,1,0:T(8,128)(2,1)}), bf16[16,88,128]{2,1,0:T(8,128)(2,1)S(1)}, u32[]{:S(2)}, u32[]{:S(2)}) async-start(bf16[16,88,128]{2,1,0:T(8,128)(2,1)} %bitcast.21), calls=%async_computation | async-start | bytes 720896 | tf_op jit(solution)/shard_map/all_to_all | solution.py:336
  10.9 0.0 copy-done.3
  10.9 0.0 copy-done.5
  10.9 0.1 multiply_reduce_fusion
  11.0 0.6 fusion.6
  11.7 0.2 convert_reduce_fusion.1
  11.9 0.1 copy.20
  12.0 0.1 select_n.54
  12.0 0.0 copy-done.2
  12.0 2.7 %collective-permute-start = (bf16[25,64,128]{2,1,0:T(8,128)(2,1)S(1)}, bf16[25,64,128]{2,1,0:T(8,128)(2,1)}, u32[]{:S(2)}, u32[]{:S(2)}) collective-permute-start(bf16[25,64,128]{2,1,0:T(8,128)(2,1)S(1)} %bitcast.18), channel_id=1, source_target_pairs={{0,1},{1,2},{2,3},{3,4},{4,5},{5,6},{6,7},{7,8},{8,9},{9,10},{10,1... | collective-permute-start | bytes 1228808 | tf_op jit(solution)/shard_map/ppermute | solution.py:361
  14.7 0.9 collective-permute-start.1
  16.2 0.0 copy-done.4
  16.3 0.1 copy.21
  16.4 0.1 reshape.81
  16.5 2.2 %all-to-all-done = bf16[16,88,128]{2,1,0:T(8,128)(2,1)S(1)} async-done(((bf16[16,88,128]{2,1,0:T(8,128)(2,1)}), bf16[16,88,128]{2,1,0:T(8,128)(2,1)S(1)}, u32[]{:S(2)}, u32[]{:S(2)}) %all-to-all-start) | async-done | bytes 360480 | tf_op jit(solution)/shard_map/all_to_all | solution.py:336
  18.7 0.1 reduce_sum.49
  18.8 1.3 %broadcast_in_dim.13 = bf16[64,88,128]{2,1,0:T(8,128)(2,1)} broadcast(bf16[88,128]{1,0:T(8,128)(2,1)S(1)} %reduce_sum.49), dimensions={1,2} | broadcast | bytes 1464320 | tf_op jit(solution)/shard_map/broadcast_in_dim | solution.py:338
  20.1 0.0 copy-start
  20.1 10.0 %all-to-all-start.1 = ((bf16[64,88,128]{2,1,0:T(8,128)(2,1)}), bf16[64,88,128]{2,1,0:T(8,128)(2,1)S(1)}, u32[]{:S(2)}, u32[]{:S(2)}) async-start(bf16[64,88,128]{2,1,0:T(8,128)(2,1)} %broadcast_in_dim.13), calls=%async_computation.1 | async-start | bytes 2883584 | tf_op jit(solution)/shard_map/all_to_all | solution.py:339
  30.1 0.0 copy-done
  30.1 0.0 copy-start.1
  30.1 1.1 %copy-done.1 = bf16[64,48,128]{2,1,0:T(8,128)(2,1)S(1)} copy-done((bf16[64,48,128]{2,1,0:T(8,128)(2,1)S(1)}, bf16[64,48,128]{2,1,0:T(8,128)(2,1)}, u32[]{:S(2)}) %copy-start.1) | copy-done | bytes 786456
  31.2 7.1 %compact_edges.1 = (f32[12,168,256]{2,1,0:T(8,128)}, f32[12,128,256]{2,1,0:T(8,128)S(1)}) custom-call(s32[12]{0:T(128)S(1)} %fusion.5.first, s32[1]{0:T(128)} %bitcast.1.tiles, s32[24,1,128]{2,1,0:T(1,128)S(1)} %bitcast.14, s32[24,1,128]{2,1,0:T(1,128)S(1)} %bitcast.15, bf16[3072,165]{1,0:T(8,128)(2,1)S(1)} %bitcast.16, bf16[3072,128]{1,0:T(8,128)(2,1)S(1)} %bitcast.17), custom_call_target="tpu_custom_call" | custom-call | flops 20000000000 | bytes 40000000 | tf_op jit(solution)/shard_map/compact_edges/pallas_call | solution.py:133
  38.4 0.0 collective-permute-done.low
  38.4 13.3 %collective-permute-done.1.high = bf16[25,64,128]{2,1,0:T(8,128)(2,1)} collective-permute-done((bf16[25,64,128]{2,1,0:T(8,128)(2,1)S(1)}, bf16[25,64,128]{2,1,0:T(8,128)(2,1)}, u32[]{:S(2)}, u32[]{:S(2)}) %collective-permute-start.1) | collective-permute-done | bytes 409632 | tf_op jit(solution)/shard_map/ppermute | solution.py:362
  51.6 16.7 %gather_rotate.1.rotated = bf16[12,3200,256]{2,1,0:T(8,128)(2,1)} custom-call(s32[1]{0:T(128)} %bitcast.1.tiles, f32[12,168,256]{2,1,0:T(8,128)} %get-tuple-element.26.frames, f32[12,128,256]{2,1,0:T(8,128)S(1)} %get-tuple-element.21.radial, bf16[25,64,128]{2,1,0:T(8,128)(2,1)S(1)} %bitcast.20, bf16[25,64,128]{2,1,0:T(8,128)(2,1)} %collective-permute-done.low, ...), custom_call_target="tpu_custom_call" | custom-call | flops 10000000000 | bytes 40000000 | tf_op jit(solution)/shard_map/gather_rotate/pallas_call | solution.py:194
  68.3 0.0 all-to-all-done.1
  68.4 0.0 collective-permute-start.2
  68.4 0.1 pad_add_fusion.info
  68.4 0.2 convert_reduce_fusion
  68.6 3.0 %collective-permute-done.2.other = bf16[5632,128]{1,0:T(8,128)(2,1)S(1)} collective-permute-done((bf16[5632,128]{1,0:T(8,128)(2,1)S(1)}, bf16[5632,128]{1,0:T(8,128)(2,1)S(1)}, u32[]{:S(2)}, u32[]{:S(2)}) %collective-permute-start.2) | collective-permute-done | bytes 1441824 | tf_op jit(solution)/shard_map/ppermute | solution.py:366
  71.6 0.1 broadcast_in_dim.16.scale
  71.6 31.4 %mix_messages.1 = f32[25,64,128]{2,1,0:T(8,128)} custom-call(s32[2]{0:T(128)S(1)} %pad_add_fusion.info, bf16[5632,128]{1,0:T(8,128)(2,1)S(1)} %bitcast.12, bf16[5632,128]{1,0:T(8,128)(2,1)S(1)} %collective-permute-done.2.other, bf16[12,3200,256]{2,1,0:T(8,128)(2,1)} %gather_rotate.1.rotated, f32[12,168,256]{2,1,0:T(8,128)} %get-tuple-element.26.frames, ...), custom_call_target="tpu_custom_call" | custom-call | flops 15000000512 | bytes 40000000 | tf_op jit(solution)/shard_map/mix_messages/pallas_call | solution.py:293
  (5 shorter events, 0.1 us)
Async XLA Ops:
  1.3 9.6 %copy-start.3 = (s32[64,64]{1,0:T(8,128)S(1)}, s32[64,64]{1,0:T(8,128)}, u32[]{:S(2)}) copy-start(s32[64,64]{1,0:T(8,128)} %constant.114.clone) | copy-start | bytes 49156
  1.3 9.6 %copy-start.5 = (s32[64]{0:T(128)S(1)}, s32[64]{0:T(128)}, u32[]{:S(2)}) copy-start(s32[64]{0:T(128)} %param.17) | copy-start | bytes 772
  1.3 10.7 %copy-start.2 = (bf16[64,25,128]{2,0,1:T(8,128)(2,1)S(1)}, bf16[64,25,128]{2,0,1:T(8,128)(2,1)}, u32[]{:S(2)}) copy-start(bf16[64,25,128]{2,0,1:T(8,128)(2,1)} %param.13) | copy-start | bytes 1228804
  1.3 14.9 %copy-start.4 = (s32[64,48]{0,1:T(8,128)S(1)}, s32[64,48]{0,1:T(8,128)}, u32[]{:S(2)}) copy-start(s32[64,48]{0,1:T(8,128)} %param.16) | copy-start | bytes 36868
  5.1 13.6 %all-to-all-start = ((bf16[16,88,128]{2,1,0:T(8,128)(2,1)}), bf16[16,88,128]{2,1,0:T(8,128)(2,1)S(1)}, u32[]{:S(2)}, u32[]{:S(2)}) async-start(bf16[16,88,128]{2,1,0:T(8,128)(2,1)} %bitcast.21), calls=%async_computation | async-start | bytes 720896 | tf_op jit(solution)/shard_map/all_to_all | solution.py:336
  12.0 26.3 %collective-permute-start = (bf16[25,64,128]{2,1,0:T(8,128)(2,1)S(1)}, bf16[25,64,128]{2,1,0:T(8,128)(2,1)}, u32[]{:S(2)}, u32[]{:S(2)}) collective-permute-start(bf16[25,64,128]{2,1,0:T(8,128)(2,1)S(1)} %bitcast.18), channel_id=1, source_target_pairs={{0,1},{1,2},{2,3},{3,4},{4,5},{5,6},{6,7},{7,8},{8,9},{9,10},{10,1... | collective-permute-start | bytes 1228808 | tf_op jit(solution)/shard_map/ppermute | solution.py:361
  14.7 36.9 %collective-permute-start.1 = (bf16[25,64,128]{2,1,0:T(8,128)(2,1)S(1)}, bf16[25,64,128]{2,1,0:T(8,128)(2,1)}, u32[]{:S(2)}, u32[]{:S(2)}) collective-permute-start(bf16[25,64,128]{2,1,0:T(8,128)(2,1)S(1)} %bitcast.19), channel_id=1, source_target_pairs={{1,0},{2,1},{3,2},{4,3},{5,4},{6,5},{7,6},{8,7},{9,8},{10,9},{11,1... | collective-permute-start | bytes 1228808 | tf_op jit(solution)/shard_map/ppermute | solution.py:362
  20.1 10.0 %copy-start = (bf16[64,48,165]{2,1,0:T(8,128)(2,1)S(1)}, bf16[64,48,165]{2,1,0:T(8,128)(2,1)}, u32[]{:S(2)}) copy-start(bf16[64,48,165]{2,1,0:T(8,128)(2,1)} %param.14) | copy-start | bytes 3041284
  20.1 48.3 %all-to-all-start.1 = ((bf16[64,88,128]{2,1,0:T(8,128)(2,1)}), bf16[64,88,128]{2,1,0:T(8,128)(2,1)S(1)}, u32[]{:S(2)}, u32[]{:S(2)}) async-start(bf16[64,88,128]{2,1,0:T(8,128)(2,1)} %broadcast_in_dim.13), calls=%async_computation.1 | async-start | bytes 2883584 | tf_op jit(solution)/shard_map/all_to_all | solution.py:339
  30.1 1.1 %copy-start.1 = (bf16[64,48,128]{2,1,0:T(8,128)(2,1)S(1)}, bf16[64,48,128]{2,1,0:T(8,128)(2,1)}, u32[]{:S(2)}) copy-start(bf16[64,48,128]{2,1,0:T(8,128)(2,1)} %param.15) | copy-start | bytes 2359300
  68.4 3.2 %collective-permute-start.2 = (bf16[5632,128]{1,0:T(8,128)(2,1)S(1)}, bf16[5632,128]{1,0:T(8,128)(2,1)S(1)}, u32[]{:S(2)}, u32[]{:S(2)}) collective-permute-start(bf16[5632,128]{1,0:T(8,128)(2,1)S(1)} %bitcast.11), channel_id=1, source_target_pairs={{0,8},{8,0},{1,9},{9,1},{2,10},{10,2},{3,11},{11,3},{4,12},{12,4},... | collective-permute-start | bytes 4325384 | tf_op jit(solution)/shard_map/ppermute | solution.py:366

commit v3 on v2

--- a/solution.py
+++ b/solution.py
@@ -14,6 +14,7 @@
 SAME_CORE = ("z", "yh", "x", "yl")
 C = 128
 TILE = 256
+STRIP = 32
 WINDOW = 1024
 BLOCKS_EACH = 11
 INDEX_LANE = 165
@@ -52,11 +53,13 @@
 
 def combine_kernel(table, coeff, w0, w1, w2, w3, w4, out, buf, sems):
     arrays = (w0, w1, w2, w3, w4)
+    mine = lax.axis_index("z") * lax.axis_size("yh") + lax.axis_index("yh")
     for j in range(BLOCKS_EACH):
-        kind = table[j, 0]
-        part = table[j, 1]
-        row = pl.multiple_of(table[j, 3] * C, C)
-        column = pl.multiple_of(table[j, 2] * C, C)
+        at = (mine * BLOCKS_EACH + j) * 4
+        kind = table[at]
+        part = table[at + 1]
+        row = pl.multiple_of(table[at + 3] * C, C)
+        column = pl.multiple_of(table[at + 2] * C, C)
         for a, ref in enumerate(arrays):
 
             @pl.when(kind == a)
@@ -166,25 +169,22 @@
     spread_frames(frames[0], spread)
     index = frames[0, INDEX_LANE : INDEX_LANE + 1, :].astype(jnp.int32)
     one_hot = (lax.broadcasted_iota(jnp.int32, (192, TILE), 0) == index).astype(jnp.float32).astype(jnp.bfloat16)
-    for q in range(25):
-        rows = slice(q * C, (q + 1) * C)
-        got = jnp.dot(table[rows, :], one_hot, preferred_element_type=jnp.float32)
-        gathered[rows, :] = (got * radial[0]).astype(jnp.bfloat16)
-
-    def channels(chunk, carried):
-        at = chunk * 16
-        offset = 0
-        for degree in range(5):
-            size = 2 * degree + 1
-            base = degree * degree
-            x = [gathered[pl.ds(pl.multiple_of((base + q) * C + at, 16), 16), :] for q in range(size)]
+    offset = 0
+    for degree in range(5):
+        size = 2 * degree + 1
+        base = degree * degree
+        for q in range(base, base + size):
+            rows = slice(q * C, (q + 1) * C)
+            got = jnp.dot(table[rows, :], one_hot, preferred_element_type=jnp.float32)
+            gathered[rows, :] = (got * radial[0]).astype(jnp.bfloat16)
+        for at in range(0, C, STRIP):
+            x = [[gathered[(base + q) * C + i : (base + q) * C + i + 16, :] for i in range(at, at + STRIP, 16)] for q in range(size)]
             for p in range(size):
-                total = tree_sum([spread[offset + p * size + q] * x[q] for q in range(size)])
-                out[0, pl.ds(pl.multiple_of(PLACE[base + p] * C + at, 16), 16), :] = total
-            offset += size * size
-        return carried
-
-    lax.fori_loop(0, 8, channels, 0)
+                entries = [spread[offset + p * size + q] for q in range(size)]
+                for k in range(STRIP // 16):
+                    row = PLACE[base + p] * C + at + 16 * k
+                    out[0, row : row + 16, :] = tree_sum([entries[q] * x[q][k] for q in range(size)])
+        offset += size * size
 
 
 def rotate(tiles, frames, radial, own, low, high):
@@ -231,7 +231,7 @@
                 put(o * C, kept + i * C, -piece)
 
 
-def mix_kernel(info, mine, other, rotated, frames, atoms, scale, out, m0, m1, m2, m3, m4, gated, message, spread, total):
+def mix_kernel(info, mine, other, rotated, frames, bounds, scale, out, m0, m1, m2, m3, m4, fresh, gated, message, spread, total):
     step = pl.program_id(0)
     mixes = (m0, m1, m2, m3, m4)
 
@@ -239,68 +239,78 @@
     def _():
         place_weights(info[0], mine, other, mixes)
         total[...] = jnp.zeros_like(total)
-
-    @pl.when(step < info[1])
-    def _():
-        mix_tile(rotated, frames, atoms, mixes, gated, message, spread, total)
-
-    @pl.when(step == pl.num_programs(0) - 1)
+        gated[...] = jnp.zeros_like(gated)
+
+    @pl.when(step <= info[1])
+    def _():
+        mix_tile(step, rotated, frames, bounds, mixes, fresh, gated, message, spread, total)
+
+    @pl.when(step == info[1])
     def _():
         for q in range(25):
-            out[q] = total[q] * scale[...]
-
-
-def mix_tile(rotated, frames, atoms, mixes, gated, message, spread, total):
-    first = jnp.dot(mixes[0][...], rotated[0, : 5 * C], preferred_element_type=jnp.float32)
-    scalar = first[:C]
-    gate = 1.0 / (1.0 + jnp.exp(-scalar))
-    for k in range(5):
-        gated[k * C : (k + 1) * C] = (first[k * C : (k + 1) * C] * gate).astype(jnp.bfloat16)
-    for order in range(1, 5):
+            out[q] = total[q * C : (q + 1) * C, :].T * scale[...]
+
+
+def mix_tile(step, rotated, frames, bounds, mixes, fresh, gated, message, spread, total):
+    edge = lax.broadcasted_iota(jnp.int32, (TILE, 64), 0) + (step - 1) * TILE
+    owned = jnp.logical_and(edge >= bounds[0:1, :], edge < bounds[1:2, :])
+    owner = owned.astype(jnp.float32).astype(jnp.bfloat16)
+    spread_frames(frames[0], spread)
+
+    def mix_order(order, gate):
         begin = START[order] * C
         size = DEPTH[order]
         mixed = jnp.dot(mixes[order][...], rotated[0, begin : begin + size * C], preferred_element_type=jnp.float32)
+        if order == 0:
+            gate = 1.0 / (1.0 + jnp.exp(-mixed[:C]))
         for k in range(size):
-            gated[begin + k * C : begin + (k + 1) * C] = (mixed[k * C : (k + 1) * C] * gate).astype(jnp.bfloat16)
-
-    spread_frames(frames[0], spread)
-
-    def channels(chunk, carried):
-        at = chunk * 16
-        offset = 0
-        for degree in range(5):
-            size = 2 * degree + 1
-            base = degree * degree
-            g = [gated[pl.ds(pl.multiple_of(PLACE[base + p] * C + at, 16), 16), :] for p in range(size)]
+            fresh[begin + k * C : begin + (k + 1) * C] = (mixed[k * C : (k + 1) * C] * gate).astype(jnp.bfloat16)
+        return gate
+
+    def turn_back(degree):
+        size = 2 * degree + 1
+        base = degree * degree
+        offset = sum((2 * d + 1) ** 2 for d in range(degree))
+        for at in range(0, C, STRIP):
+            g = [
+                [gated[PLACE[base + p] * C + i : PLACE[base + p] * C + i + 16, :] for i in range(at, at + STRIP, 16)]
+                for p in range(size)
+            ]
             for q in range(size):
-                value = tree_sum([spread[offset + p * size + q] * g[p] for p in range(size)])
-                message[pl.ds(pl.multiple_of((base + q) * C + at, 16), 16), :] = value
-            offset += size * size
-        return carried
-
-    lax.fori_loop(0, 8, channels, 0)
-
-    owner = (lax.broadcasted_iota(jnp.int32, (64, TILE), 0) == atoms[0]).astype(jnp.float32).astype(jnp.bfloat16)
-    for q in range(25):
-        total[q] += lax.dot_general(
-            owner, message[q * C : (q + 1) * C, :], (((1,), (1,)), ((), ())), preferred_element_type=jnp.float32
-        )
-
-
-def mix(info, mine, other, rotated, frames, atoms, scale):
+                entries = [spread[offset + p * size + q] for p in range(size)]
+                for k in range(STRIP // 16):
+                    row = (base + q) * C + at + 16 * k
+                    message[row : row + 16, :] = tree_sum([entries[p] * g[p][k] for p in range(size)])
+        rows = slice(base * C, (base + size) * C)
+        total[rows, :] += jnp.dot(message[rows, :], owner, preferred_element_type=jnp.float32)
+
+    gate = mix_order(0, None)
+    turn_back(4)
+    mix_order(1, gate)
+    turn_back(3)
+    mix_order(2, gate)
+    turn_back(2)
+    mix_order(3, gate)
+    turn_back(1)
+    mix_order(4, gate)
+    turn_back(0)
+    gated[...] = fresh[...]
+
+
+def mix(info, mine, other, rotated, frames, bounds, scale):
     whole = lambda *shape: pl.BlockSpec(shape, lambda i, *_: (0,) * len(shape))
-    block = lambda a: pl.BlockSpec((1,) + a.shape[1:], lambda i, n: (jnp.minimum(i, n[1] - 1), 0, 0))
+    block = lambda a, lag: pl.BlockSpec((1,) + a.shape[1:], lambda i, n: (jnp.clip(i - lag, 0, n[1] - 1), 0, 0))
     return pl.pallas_call(
         mix_kernel,
         grid_spec=pltpu.PrefetchScalarGridSpec(
             num_scalar_prefetch=1,
-            grid=(rotated.shape[0],),
+            grid=(rotated.shape[0] + 1,),
             in_specs=[
                 whole(*mine.shape),
                 whole(*other.shape),
-                block(rotated),
-                block(frames),
-                block(atoms),
+                block(rotated, 0),
+                block(frames, 1),
+                whole(*bounds.shape),
                 whole(*scale.shape),
             ],
             out_specs=whole(25, 64, C),
@@ -308,15 +318,16 @@
             + [
                 pltpu.VMEM((25 * C, TILE), jnp.bfloat16),
                 pltpu.VMEM((25 * C, TILE), jnp.bfloat16),
+                pltpu.VMEM((25 * C, TILE), jnp.bfloat16),
                 pltpu.VMEM((INDEX_LANE, 16, TILE), jnp.bfloat16),
-                pltpu.VMEM((25, 64, C), jnp.float32),
+                pltpu.VMEM((25 * C, 64), jnp.float32),
             ],
         ),
         out_shape=jax.ShapeDtypeStruct((25, 64, C), jnp.float32),
         compiler_params=pltpu.CompilerParams(vmem_limit_bytes=VMEM),
         cost_estimate=pl.CostEstimate(flops=15 * 10**9, bytes_accessed=40 * 10**6, transcendentals=10**6),
         name="mix_messages",
-    )(info, mine, other, rotated, frames, atoms, scale)
+    )(info, mine, other, rotated, frames, bounds, scale)
 
 
 def body(sizes, node_features, frames, radial, neighbours, counts, coefficients, *weights):
@@ -328,10 +339,8 @@
     n_narrow = sizes["z"] * sizes["yh"]
     n_xy = sizes["x"] * sizes["yl"]
 
-    narrow = lax.axis_index(NARROW)
     rows = np.array([BLOCKS[min(g, len(BLOCKS) - 1)] for g in range(n_narrow * BLOCKS_EACH)], np.int32)
-    table = lax.dynamic_slice_in_dim(jnp.asarray(rows), narrow * BLOCKS_EACH, BLOCKS_EACH, 0)
-    partial = combine(table, coefficients, weights)
+    partial = combine(jnp.asarray(rows.reshape(-1)), coefficients, weights)
     share_rows = partial.shape[1] // n_xy
     parts = lax.all_to_all(partial.reshape(-1, share_rows, C), ("core", "x", "yl"), 0, 0, tiled=True)
     share = jnp.sum(parts.astype(jnp.float32), axis=0).astype(jnp.bfloat16)
@@ -346,8 +355,6 @@
     ends = offset + counts
     slot = lax.broadcasted_iota(jnp.int32, (atoms_here, slots), 1)
     position = jnp.where(slot < counts[:, None], offset[:, None] + slot, -1).reshape(edges // C, 1, C)
-    places = jnp.arange(edges, dtype=jnp.int32)
-    atoms = jnp.sum((ends[None, :] <= places[:, None]).astype(jnp.int32), axis=1)
     starts = jnp.arange(most, dtype=jnp.int32) * TILE
     first_atom = jnp.sum((ends[None, :] <= starts[:, None]).astype(jnp.int32), axis=1)
     first = jnp.minimum(first_atom * slots // C, (edges - WINDOW) // C)
@@ -366,7 +373,7 @@
     other = lax.ppermute(mine, "core", [(0, 1), (1, 0)])
     scale = jnp.broadcast_to(1.0 / jnp.sqrt(counts.astype(jnp.float32))[:, None], (atoms_here, C))
     info = jnp.concatenate([lax.axis_index("core").astype(jnp.int32).reshape(1), tiles])
-    out = mix(info, mine, other, rotated, turned, atoms.reshape(most, 1, TILE), scale)
+    out = mix(info, mine, other, rotated, turned, jnp.stack([offset, ends]), scale)
     return out.transpose(1, 0, 2)
 
 

time: 104 us -> 93.1 us (0.90)
  the two profiles are of different devices: /device:TPU:56 before, /device:TPU:25 now
where the time goes in v3:
time: 93.1 us; the launch traced here: 92.3 us
  Pallas kernels  49.9 us (54%)
  starting transfers between devices  23.8 us (26%)
  waiting for transfers between devices  13.9 us (15%)
  local copies, waits for them, and re-layouts  2.83 us (3%)
  other arithmetic  1.17 us (1%)
    pallas_call x1, Pallas kernels, mix(): pl.pallas_call(mix_kernel, grid_spec=pltpu.PrefetchScalarGridSpec(num_sca...  25 us
    pallas_call x1, Pallas kernels, rotate(): pl.pallas_call(rotate_kernel, grid_spec=pltpu.PrefetchScalarGridSpec(num_...  14.1 us
    all_to_all x1, starting transfers between devices, body(): mine = lax.all_to_all(copies, SAME_CORE, 0, 0, tiled=True).reshape(-1, C)  9.81 us
    ppermute x1, waiting for transfers between devices, body(): high = lax.ppermute(own, ATOM_AXES, [(b, a) for a, b in up])  8.73 us
    pallas_call x1, Pallas kernels, compact(): pl.pallas_call(compact_kernel, grid_spec=pltpu.PrefetchScalarGridSpec(num...  7.15 us
    all_to_all x1, starting transfers between devices, body(): lax.all_to_all(partial.reshape(-1, share_rows, C), ('core', 'x', 'yl'), 0...  6.1 us
    ppermute x1, starting transfers between devices, body(): other = lax.ppermute(mine, 'core', [(0, 1), (1, 0)])  4.86 us
    pallas_call x1, Pallas kernels, combine(): pl.pallas_call(combine_kernel, grid_spec=pltpu.PrefetchScalarGridSpec(num...  3.7 us
  transfers between devices with their start and end apart: 5, of which 3 were waited for; matrix products, arithmetic and copies ran while one was open for 3% of the time, Pallas kernels for 23%

profile of v3, /device:TPU:25, one launch (start us, length us, event | category | flops | bytes accessed | tf_op | source)
XLA Modules:
  0.0 92.3 jit_solution(502757431033907005)
XLA Ops:
  0.0 0.0 copy-start.3
  0.0 0.0 copy-start.5
  0.0 0.0 copy-start.2
  0.0 0.0 copy-start.4
  0.0 3.7 %merge_group.1 = bf16[2,704,128]{2,1,0:T(8,128)(2,1)} custom-call(s32[352]{0:T(512)} %constant.109.clone.table, f32[2]{0:T(128)} %coeff.1, bf16[2,640,640]{2,1,0:T(8,128)(2,1)} %w0.1, bf16[2,2,512,512]{3,2,1,0:T(8,128)(2,1)} %w1.1, bf16[2,2,384,384]{3,2,1,0:T(8,128)(2,1)} %w2.1, bf16[2,2,256,256]{3,2,1,0:T(8,128)(2,1)} %w3.1, bf16[2,2,128,128]{3,2,1,0:T(8,128)(2,1)} %w4.1), custom_call_target="tpu_custom_call" | custom-call | flops 720896 | bytes 1081344 | tf_op jit(solution)/shard_map/merge_group/pallas_call | solution.py:82
  3.7 6.1 %all-to-all-start = ((bf16[16,88,128]{2,1,0:T(8,128)(2,1)}), bf16[16,88,128]{2,1,0:T(8,128)(2,1)S(1)}, u32[]{:S(2)}, u32[]{:S(2)}) async-start(bf16[16,88,128]{2,1,0:T(8,128)(2,1)} %bitcast.21), calls=%async_computation | async-start | bytes 720896 | tf_op jit(solution)/shard_map/all_to_all | solution.py:345
  9.8 0.0 copy-done.3
  9.8 0.0 copy-done.5
  9.9 0.1 multiply_reduce_fusion
  10.0 0.7 fusion.6
  10.6 0.2 convert_reduce_fusion
  10.8 0.1 copy.20
  10.9 0.1 select_n.50
  11.0 0.0 copy-done.2
  11.0 2.4 %collective-permute-start = (bf16[25,64,128]{2,1,0:T(8,128)(2,1)S(1)}, bf16[25,64,128]{2,1,0:T(8,128)(2,1)}, u32[]{:S(2)}, u32[]{:S(2)}) collective-permute-start(bf16[25,64,128]{2,1,0:T(8,128)(2,1)S(1)} %bitcast.18), channel_id=1, source_target_pairs={{0,1},{1,2},{2,3},{3,4},{4,5},{5,6},{6,7},{7,8},{8,9},{9,10},{10,1... | collective-permute-start | bytes 1228808 | tf_op jit(solution)/shard_map/ppermute | solution.py:368
  13.4 0.7 collective-permute-start.1
  14.7 0.0 copy-done.4
  14.7 0.1 copy.21
  14.8 0.1 reshape.78
  14.9 2.4 %all-to-all-done = bf16[16,88,128]{2,1,0:T(8,128)(2,1)S(1)} async-done(((bf16[16,88,128]{2,1,0:T(8,128)(2,1)}), bf16[16,88,128]{2,1,0:T(8,128)(2,1)S(1)}, u32[]{:S(2)}, u32[]{:S(2)}) %all-to-all-start) | async-done | bytes 360480 | tf_op jit(solution)/shard_map/all_to_all | solution.py:345
  17.3 0.1 reduce_sum.40
  17.4 1.3 %broadcast_in_dim.16 = bf16[64,88,128]{2,1,0:T(8,128)(2,1)} broadcast(bf16[88,128]{1,0:T(8,128)(2,1)S(1)} %reduce_sum.40), dimensions={1,2} | broadcast | bytes 1464320 | tf_op jit(solution)/shard_map/broadcast_in_dim | solution.py:347
  18.7 0.0 copy-start
  18.7 9.8 %all-to-all-start.1 = ((bf16[64,88,128]{2,1,0:T(8,128)(2,1)}), bf16[64,88,128]{2,1,0:T(8,128)(2,1)S(1)}, u32[]{:S(2)}, u32[]{:S(2)}) async-start(bf16[64,88,128]{2,1,0:T(8,128)(2,1)} %broadcast_in_dim.16), calls=%async_computation.1 | async-start | bytes 2883584 | tf_op jit(solution)/shard_map/all_to_all | solution.py:348
  28.5 0.0 copy-done
  28.5 0.0 copy-start.1
  28.5 1.1 %copy-done.1 = bf16[64,48,128]{2,1,0:T(8,128)(2,1)S(1)} copy-done((bf16[64,48,128]{2,1,0:T(8,128)(2,1)S(1)}, bf16[64,48,128]{2,1,0:T(8,128)(2,1)}, u32[]{:S(2)}) %copy-start.1) | copy-done | bytes 786456
  29.6 7.1 %compact_edges.1 = (f32[12,168,256]{2,1,0:T(8,128)}, f32[12,128,256]{2,1,0:T(8,128)S(1)}) custom-call(s32[12]{0:T(128)S(1)} %fusion.5.first, s32[1]{0:T(128)} %bitcast.1.tiles, s32[24,1,128]{2,1,0:T(1,128)S(1)} %bitcast.14, s32[24,1,128]{2,1,0:T(1,128)S(1)} %bitcast.15, bf16[3072,165]{1,0:T(8,128)(2,1)S(1)} %bitcast.16, bf16[3072,128]{1,0:T(8,128)(2,1)S(1)} %bitcast.17), custom_call_target="tpu_custom_call" | custom-call | flops 20000000000 | bytes 40000000 | tf_op jit(solution)/shard_map/compact_edges/pallas_call | solution.py:136
  36.8 0.0 collective-permute-done.low
  36.8 8.7 %collective-permute-done.1.high = bf16[25,64,128]{2,1,0:T(8,128)(2,1)} collective-permute-done((bf16[25,64,128]{2,1,0:T(8,128)(2,1)S(1)}, bf16[25,64,128]{2,1,0:T(8,128)(2,1)}, u32[]{:S(2)}, u32[]{:S(2)}) %collective-permute-start.1) | collective-permute-done | bytes 409632 | tf_op jit(solution)/shard_map/ppermute | solution.py:369
  45.5 14.1 %gather_rotate.1.rotated = bf16[12,3200,256]{2,1,0:T(8,128)(2,1)} custom-call(s32[1]{0:T(128)} %bitcast.1.tiles, f32[12,168,256]{2,1,0:T(8,128)} %get-tuple-element.26.frames, f32[12,128,256]{2,1,0:T(8,128)S(1)} %get-tuple-element.21.radial, bf16[25,64,128]{2,1,0:T(8,128)(2,1)S(1)} %bitcast.20, bf16[25,64,128]{2,1,0:T(8,128)(2,1)} %collective-permute-done.low, ...), custom_call_target="tpu_custom_call" | custom-call | flops 10000000000 | bytes 40000000 | tf_op jit(solution)/shard_map/gather_rotate/pallas_call | solution.py:194
  59.6 0.0 all-to-all-done.1
  59.6 4.9 %collective-permute-start.2 = (bf16[5632,128]{1,0:T(8,128)(2,1)S(1)}, bf16[5632,128]{1,0:T(8,128)(2,1)S(1)}, u32[]{:S(2)}, u32[]{:S(2)}) collective-permute-start(bf16[5632,128]{1,0:T(8,128)(2,1)S(1)} %bitcast.12), channel_id=1, source_target_pairs={{0,8},{8,0},{1,9},{9,1},{2,10},{10,2},{3,11},{11,3},{4,12},{12,4},... | collective-permute-start | bytes 4325384 | tf_op jit(solution)/shard_map/ppermute | solution.py:373
  64.5 0.1 pad_add_fusion.1.info
  64.5 2.8 %collective-permute-done.2.other = bf16[5632,128]{1,0:T(8,128)(2,1)S(1)} collective-permute-done((bf16[5632,128]{1,0:T(8,128)(2,1)S(1)}, bf16[5632,128]{1,0:T(8,128)(2,1)S(1)}, u32[]{:S(2)}, u32[]{:S(2)}) %collective-permute-start.2) | collective-permute-done | bytes 1441824 | tf_op jit(solution)/shard_map/ppermute | solution.py:373
  67.3 0.1 broadcast_in_dim.19.scale
  67.4 25.0 %mix_messages.1 = f32[25,64,128]{2,1,0:T(8,128)} custom-call(s32[2]{0:T(128)S(1)} %pad_add_fusion.1.info, bf16[5632,128]{1,0:T(8,128)(2,1)S(1)} %bitcast.13, bf16[5632,128]{1,0:T(8,128)(2,1)S(1)} %collective-permute-done.2.other, bf16[12,3200,256]{2,1,0:T(8,128)(2,1)} %gather_rotate.1.rotated, f32[12,168,256]{2,1,0:T(8,128)} %get-tuple-element.26.frames, ...), custom_call_target="tpu_custom_call" | custom-call | flops 15000000512 | bytes 40000000 | tf_op jit(solution)/shard_map/mix_messages/pallas_call | solution.py:303
  (6 shorter events, 0.1 us)
Async XLA Ops:
  0.0 9.8 %copy-start.3 = (s32[64,64]{1,0:T(8,128)S(1)}, s32[64,64]{1,0:T(8,128)}, u32[]{:S(2)}) copy-start(s32[64,64]{1,0:T(8,128)} %constant.110.clone) | copy-start | bytes 49156
  0.0 9.8 %copy-start.5 = (s32[64]{0:T(128)S(1)}, s32[64]{0:T(128)}, u32[]{:S(2)}) copy-start(s32[64]{0:T(128)} %param.17) | copy-start | bytes 772
  0.0 11.0 %copy-start.2 = (bf16[64,25,128]{2,0,1:T(8,128)(2,1)S(1)}, bf16[64,25,128]{2,0,1:T(8,128)(2,1)}, u32[]{:S(2)}) copy-start(bf16[64,25,128]{2,0,1:T(8,128)(2,1)} %param.13) | copy-start | bytes 1228804
  0.0 14.7 %copy-start.4 = (s32[64,48]{0,1:T(8,128)S(1)}, s32[64,48]{0,1:T(8,128)}, u32[]{:S(2)}) copy-start(s32[64,48]{0,1:T(8,128)} %param.16) | copy-start | bytes 36868
  3.7 13.6 %all-to-all-start = ((bf16[16,88,128]{2,1,0:T(8,128)(2,1)}), bf16[16,88,128]{2,1,0:T(8,128)(2,1)S(1)}, u32[]{:S(2)}, u32[]{:S(2)}) async-start(bf16[16,88,128]{2,1,0:T(8,128)(2,1)} %bitcast.21), calls=%async_computation | async-start | bytes 720896 | tf_op jit(solution)/shard_map/all_to_all | solution.py:345
  11.0 25.8 %collective-permute-start = (bf16[25,64,128]{2,1,0:T(8,128)(2,1)S(1)}, bf16[25,64,128]{2,1,0:T(8,128)(2,1)}, u32[]{:S(2)}, u32[]{:S(2)}) collective-permute-start(bf16[25,64,128]{2,1,0:T(8,128)(2,1)S(1)} %bitcast.18), channel_id=1, source_target_pairs={{0,1},{1,2},{2,3},{3,4},{4,5},{5,6},{6,7},{7,8},{8,9},{9,10},{10,1... | collective-permute-start | bytes 1228808 | tf_op jit(solution)/shard_map/ppermute | solution.py:368
  13.4 32.1 %collective-permute-start.1 = (bf16[25,64,128]{2,1,0:T(8,128)(2,1)S(1)}, bf16[25,64,128]{2,1,0:T(8,128)(2,1)}, u32[]{:S(2)}, u32[]{:S(2)}) collective-permute-start(bf16[25,64,128]{2,1,0:T(8,128)(2,1)S(1)} %bitcast.19), channel_id=1, source_target_pairs={{1,0},{2,1},{3,2},{4,3},{5,4},{6,5},{7,6},{8,7},{9,8},{10,9},{11,1... | collective-permute-start | bytes 1228808 | tf_op jit(solution)/shard_map/ppermute | solution.py:369
  18.7 9.8 %copy-start = (bf16[64,48,165]{2,1,0:T(8,128)(2,1)S(1)}, bf16[64,48,165]{2,1,0:T(8,128)(2,1)}, u32[]{:S(2)}) copy-start(bf16[64,48,165]{2,1,0:T(8,128)(2,1)} %param.14) | copy-start | bytes 3041284
  18.7 40.9 %all-to-all-start.1 = ((bf16[64,88,128]{2,1,0:T(8,128)(2,1)}), bf16[64,88,128]{2,1,0:T(8,128)(2,1)S(1)}, u32[]{:S(2)}, u32[]{:S(2)}) async-start(bf16[64,88,128]{2,1,0:T(8,128)(2,1)} %broadcast_in_dim.16), calls=%async_computation.1 | async-start | bytes 2883584 | tf_op jit(solution)/shard_map/all_to_all | solution.py:348
  28.5 1.1 %copy-start.1 = (bf16[64,48,128]{2,1,0:T(8,128)(2,1)S(1)}, bf16[64,48,128]{2,1,0:T(8,128)(2,1)}, u32[]{:S(2)}) copy-start(bf16[64,48,128]{2,1,0:T(8,128)(2,1)} %param.15) | copy-start | bytes 2359300
  59.6 7.7 %collective-permute-start.2 = (bf16[5632,128]{1,0:T(8,128)(2,1)S(1)}, bf16[5632,128]{1,0:T(8,128)(2,1)S(1)}, u32[]{:S(2)}, u32[]{:S(2)}) collective-permute-start(bf16[5632,128]{1,0:T(8,128)(2,1)S(1)} %bitcast.12), channel_id=1, source_target_pairs={{0,8},{8,0},{1,9},{9,1},{2,10},{10,2},{3,11},{11,3},{4,12},{12,4},... | collective-permute-start | bytes 4325384 | tf_op jit(solution)/shard_map/ppermute | solution.py:373

commit v4 on v3

--- a/solution.py
+++ b/solution.py
@@ -20,6 +20,7 @@
 INDEX_LANE = 165
 DEPTH = (5, 8, 6, 4, 2)
 START = (0, 5, 13, 19, 23)
+THREE = (1, 3)
 VMEM = 100 * 2**20 // 2
 
 
@@ -211,8 +212,28 @@
     )(tiles, frames, radial, own, low, high)
 
 
+def mix_shape(order):
+    size = DEPTH[order] * C
+    return (3, size // 2, size // 2) if order in THREE else (size, size)
+
+
 def place_weights(core, mine, other, mixes):
+    where = {block: g for g, block in enumerate(BLOCKS)}
     for g, (order, part, o, i) in enumerate(BLOCKS):
+        if order in THREE:
+            if part == 0:
+                pair = where[order, 1, o, i]
+                for half, ref in ((core, mine), (1 - core, other)):
+                    real = ref[64 * g : 64 * g + 64, :]
+                    imag = ref[64 * pair : 64 * pair + 64, :]
+                    wide_real = real.astype(jnp.float32)
+                    wide_imag = imag.astype(jnp.float32)
+                    rows = pl.ds(pl.multiple_of(o * C + half * 64, 64), 64)
+                    columns = slice(i * C, (i + 1) * C)
+                    mixes[order][0, rows, columns] = real
+                    mixes[order][1, rows, columns] = (wide_imag - wide_real).astype(jnp.bfloat16)
+                    mixes[order][2, rows, columns] = (wide_real + wide_imag).astype(jnp.bfloat16)
+            continue
         kept = C * DEPTH[order] // 2
         for half, ref in ((core, mine), (1 - core, other)):
             piece = ref[64 * g : 64 * g + 64, :]
@@ -260,6 +281,20 @@
     def mix_order(order, gate):
         begin = START[order] * C
         size = DEPTH[order]
+        if order in THREE:
+            half = size * C // 2
+            plus = rotated[0, begin : begin + half]
+            minus = rotated[0, begin + half : begin + size * C]
+            dot = lambda k, x: jnp.dot(mixes[order][k], x, preferred_element_type=jnp.float32)
+            shared = dot(0, plus + minus)
+            up = shared - dot(2, minus)
+            for k in range(size // 2):
+                fresh[begin + k * C : begin + (k + 1) * C] = (up[k * C : (k + 1) * C] * gate).astype(jnp.bfloat16)
+            down = shared + dot(1, plus)
+            for k in range(size // 2):
+                at = begin + half + k * C
+                fresh[at : at + C] = (down[k * C : (k + 1) * C] * gate).astype(jnp.bfloat16)
+            return gate
         mixed = jnp.dot(mixes[order][...], rotated[0, begin : begin + size * C], preferred_element_type=jnp.float32)
         if order == 0:
             gate = 1.0 / (1.0 + jnp.exp(-mixed[:C]))
@@ -314,7 +349,7 @@
                 whole(*scale.shape),
             ],
             out_specs=whole(25, 64, C),
-            scratch_shapes=[pltpu.VMEM((d * C, d * C), jnp.bfloat16) for d in DEPTH]
+            scratch_shapes=[pltpu.VMEM(mix_shape(order), jnp.bfloat16) for order in range(5)]
             + [
                 pltpu.VMEM((25 * C, TILE), jnp.bfloat16),
                 pltpu.VMEM((25 * C, TILE), jnp.bfloat16),
@@ -366,7 +401,7 @@
     )
     up = [(i, (i + 1) % devices) for i in range(devices)]
     low = lax.ppermute(own, ATOM_AXES, up)
-    high = lax.ppermute(own, ATOM_AXES, [(b, a) for a, b in up])
+    high = lax.ppermute(node_features.transpose(1, 0, 2), ATOM_AXES, [(b, a) for a, b in up])
     turned, low, high = lax.optimization_barrier((turned, low, high))
     rotated = rotate(tiles, turned, factor, own, low, high)
     mine, rotated, turned = lax.optimization_barrier((mine, rotated, turned))

time: 93.1 us -> 82.1 us (0.88)
  the two profiles are of different devices: /device:TPU:25 before, /device:TPU:1 now
where the time goes in v4:
time: 82.1 us
  Pallas kernels  49.4 us (60%)
  starting transfers between devices  19.1 us (23%)
  waiting for transfers between devices  8.82 us (11%)
  local copies, waits for them, and re-layouts  2.83 us (3%)
  other arithmetic  1.17 us (1%)
    pallas_call x1, Pallas kernels, mix(): pl.pallas_call(mix_kernel, grid_spec=pltpu.PrefetchScalarGridSpec(num_sca...  24.2 us
    pallas_call x1, Pallas kernels, rotate(): pl.pallas_call(rotate_kernel, grid_spec=pltpu.PrefetchScalarGridSpec(num_...  14.5 us
    ppermute x1, starting transfers between devices, body(): lax.ppermute(node_features.transpose(1, 0, 2), ATOM_AXES, [(b, a) for a,...  7.86 us
    pallas_call x1, Pallas kernels, compact(): pl.pallas_call(compact_kernel, grid_spec=pltpu.PrefetchScalarGridSpec(num...  7.15 us
    all_to_all x1, waiting for transfers between devices, body(): lax.all_to_all(partial.reshape(-1, share_rows, C), ('core', 'x', 'yl'), 0...  6.05 us
    all_to_all x1, starting transfers between devices, body(): lax.all_to_all(partial.reshape(-1, share_rows, C), ('core', 'x', 'yl'), 0...  5.25 us
    all_to_all x1, starting transfers between devices, body(): mine = lax.all_to_all(copies, SAME_CORE, 0, 0, tiled=True).reshape(-1, C)  4.8 us
    pallas_call x1, Pallas kernels, combine(): pl.pallas_call(combine_kernel, grid_spec=pltpu.PrefetchScalarGridSpec(num...  3.56 us
  transfers between devices with their start and end apart: 5, of which 2 were waited for; matrix products, arithmetic and copies ran while one was open for 3% of the time, Pallas kernels for 31%

profile of v4, /device:TPU:1, one launch (start us, length us, event | category | flops | bytes accessed | tf_op | source)
XLA Modules:
  0.0 82.1 jit_solution(12940806880696509932)
XLA Ops:
  0.0 0.0 copy-start.3
  0.0 0.0 copy-start.5
  0.0 0.0 copy-start.2
  0.0 0.0 copy-start.4
  0.0 7.9 %collective-permute-start.1 = (bf16[25,64,128]{2,1,0:T(8,128)(2,1)}, bf16[25,64,128]{2,1,0:T(8,128)(2,1)}, u32[]{:S(2)}, u32[]{:S(2)}) collective-permute-start(bf16[25,64,128]{2,1,0:T(8,128)(2,1)} %bitcast.18), channel_id=1, source_target_pairs={{1,0},{2,1},{3,2},{4,3},{5,4},{6,5},{7,6},{8,7},{9,8},{10,9},{11,1... | collective-permute-start | bytes 1228808 | tf_op jit(solution)/shard_map/ppermute | solution.py:404
  7.9 3.6 %merge_group.1 = bf16[2,704,128]{2,1,0:T(8,128)(2,1)} custom-call(s32[352]{0:T(512)} %constant.109.clone.table, f32[2]{0:T(128)} %coeff.1, bf16[2,640,640]{2,1,0:T(8,128)(2,1)} %w0.1, bf16[2,2,512,512]{3,2,1,0:T(8,128)(2,1)} %w1.1, bf16[2,2,384,384]{3,2,1,0:T(8,128)(2,1)} %w2.1, bf16[2,2,256,256]{3,2,1,0:T(8,128)(2,1)} %w3.1, bf16[2,2,128,128]{3,2,1,0:T(8,128)(2,1)} %w4.1), custom_call_target="tpu_custom_call" | custom-call | flops 720896 | bytes 1081344 | tf_op jit(solution)/shard_map/merge_group/pallas_call | solution.py:83
  11.4 5.2 %all-to-all-start = ((bf16[16,88,128]{2,1,0:T(8,128)(2,1)}), bf16[16,88,128]{2,1,0:T(8,128)(2,1)S(1)}, u32[]{:S(2)}, u32[]{:S(2)}) async-start(bf16[16,88,128]{2,1,0:T(8,128)(2,1)} %bitcast.21), calls=%async_computation | async-start | bytes 720896 | tf_op jit(solution)/shard_map/all_to_all | solution.py:380
  16.7 0.0 copy-done.3
  16.7 0.0 copy-done.5
  16.7 0.1 multiply_reduce_fusion
  16.8 0.7 fusion.6
  17.5 0.2 convert_reduce_fusion
  17.7 0.1 copy.20
  17.8 0.1 select_n.50
  17.9 0.0 copy-done.2
  17.9 0.1 collective-permute-start
  18.6 0.0 copy-done.4
  18.7 0.1 copy.21
  18.7 0.1 reshape.78
  18.8 6.0 %all-to-all-done = bf16[16,88,128]{2,1,0:T(8,128)(2,1)S(1)} async-done(((bf16[16,88,128]{2,1,0:T(8,128)(2,1)}), bf16[16,88,128]{2,1,0:T(8,128)(2,1)S(1)}, u32[]{:S(2)}, u32[]{:S(2)}) %all-to-all-start) | async-done | bytes 360480 | tf_op jit(solution)/shard_map/all_to_all | solution.py:380
  24.9 0.1 reduce_sum.40
  24.9 1.3 %broadcast_in_dim.16 = bf16[64,88,128]{2,1,0:T(8,128)(2,1)} broadcast(bf16[88,128]{1,0:T(8,128)(2,1)S(1)} %reduce_sum.40), dimensions={1,2} | broadcast | bytes 1464320 | tf_op jit(solution)/shard_map/broadcast_in_dim | solution.py:382
  26.2 0.0 copy-start
  26.2 4.8 %all-to-all-start.1 = ((bf16[64,88,128]{2,1,0:T(8,128)(2,1)}), bf16[64,88,128]{2,1,0:T(8,128)(2,1)S(1)}, u32[]{:S(2)}, u32[]{:S(2)}) async-start(bf16[64,88,128]{2,1,0:T(8,128)(2,1)} %broadcast_in_dim.16), calls=%async_computation.1 | async-start | bytes 2883584 | tf_op jit(solution)/shard_map/all_to_all | solution.py:383
  31.0 0.0 copy-done
  31.0 0.0 copy-start.1
  31.1 1.1 %copy-done.1 = bf16[64,48,128]{2,1,0:T(8,128)(2,1)S(1)} copy-done((bf16[64,48,128]{2,1,0:T(8,128)(2,1)S(1)}, bf16[64,48,128]{2,1,0:T(8,128)(2,1)}, u32[]{:S(2)}) %copy-start.1) | copy-done | bytes 786456
  32.2 7.2 %compact_edges.1 = (f32[12,168,256]{2,1,0:T(8,128)}, f32[12,128,256]{2,1,0:T(8,128)S(1)}) custom-call(s32[12]{0:T(128)S(1)} %fusion.5.first, s32[1]{0:T(128)} %bitcast.1.tiles, s32[24,1,128]{2,1,0:T(1,128)S(1)} %bitcast.14, s32[24,1,128]{2,1,0:T(1,128)S(1)} %bitcast.15, bf16[3072,165]{1,0:T(8,128)(2,1)S(1)} %bitcast.16, bf16[3072,128]{1,0:T(8,128)(2,1)S(1)} %bitcast.17), custom_call_target="tpu_custom_call" | custom-call | flops 20000000000 | bytes 40000000 | tf_op jit(solution)/shard_map/compact_edges/pallas_call | solution.py:137
  39.3 0.0 collective-permute-done.low
  39.3 0.0 collective-permute-done.1.high
  39.3 14.5 %gather_rotate.1.rotated = bf16[12,3200,256]{2,1,0:T(8,128)(2,1)} custom-call(s32[1]{0:T(128)} %bitcast.1.tiles, f32[12,168,256]{2,1,0:T(8,128)} %get-tuple-element.26.frames, f32[12,128,256]{2,1,0:T(8,128)S(1)} %get-tuple-element.21.radial, bf16[25,64,128]{2,1,0:T(8,128)(2,1)S(1)} %bitcast.20, bf16[25,64,128]{2,1,0:T(8,128)(2,1)} %collective-permute-done.low, ...), custom_call_target="tpu_custom_call" | custom-call | flops 10000000000 | bytes 40000000 | tf_op jit(solution)/shard_map/gather_rotate/pallas_call | solution.py:195
  53.8 0.0 all-to-all-done.1
  53.8 1.1 %collective-permute-start.2 = (bf16[5632,128]{1,0:T(8,128)(2,1)S(1)}, bf16[5632,128]{1,0:T(8,128)(2,1)S(1)}, u32[]{:S(2)}, u32[]{:S(2)}) collective-permute-start(bf16[5632,128]{1,0:T(8,128)(2,1)S(1)} %bitcast.12), channel_id=1, source_target_pairs={{0,8},{8,0},{1,9},{9,1},{2,10},{10,2},{3,11},{11,3},{4,12},{12,4},... | collective-permute-start | bytes 4325384 | tf_op jit(solution)/shard_map/ppermute | solution.py:408
  55.0 0.1 pad_add_fusion.1.info
  55.0 2.8 %collective-permute-done.2.other = bf16[5632,128]{1,0:T(8,128)(2,1)S(1)} collective-permute-done((bf16[5632,128]{1,0:T(8,128)(2,1)S(1)}, bf16[5632,128]{1,0:T(8,128)(2,1)S(1)}, u32[]{:S(2)}, u32[]{:S(2)}) %collective-permute-start.2) | collective-permute-done | bytes 1441824 | tf_op jit(solution)/shard_map/ppermute | solution.py:408
  57.8 0.1 broadcast_in_dim.19.scale
  57.9 24.2 %mix_messages.1 = f32[25,64,128]{2,1,0:T(8,128)} custom-call(s32[2]{0:T(128)S(1)} %pad_add_fusion.1.info, bf16[5632,128]{1,0:T(8,128)(2,1)S(1)} %bitcast.13, bf16[5632,128]{1,0:T(8,128)(2,1)S(1)} %collective-permute-done.2.other, bf16[12,3200,256]{2,1,0:T(8,128)(2,1)} %gather_rotate.1.rotated, f32[12,168,256]{2,1,0:T(8,128)} %get-tuple-element.26.frames, ...), custom_call_target="tpu_custom_call" | custom-call | flops 15000000512 | bytes 40000000 | tf_op jit(solution)/shard_map/mix_messages/pallas_call | solution.py:338
  (6 shorter events, 0.1 us)
Async XLA Ops:
  0.0 16.7 %copy-start.3 = (s32[64,64]{1,0:T(8,128)S(1)}, s32[64,64]{1,0:T(8,128)}, u32[]{:S(2)}) copy-start(s32[64,64]{1,0:T(8,128)} %constant.110.clone) | copy-start | bytes 49156
  0.0 16.7 %copy-start.5 = (s32[64]{0:T(128)S(1)}, s32[64]{0:T(128)}, u32[]{:S(2)}) copy-start(s32[64]{0:T(128)} %param.17) | copy-start | bytes 772
  0.0 17.9 %copy-start.2 = (bf16[64,25,128]{2,0,1:T(8,128)(2,1)S(1)}, bf16[64,25,128]{2,0,1:T(8,128)(2,1)}, u32[]{:S(2)}) copy-start(bf16[64,25,128]{2,0,1:T(8,128)(2,1)} %param.13) | copy-start | bytes 1228804
  0.0 18.6 %copy-start.4 = (s32[64,48]{0,1:T(8,128)S(1)}, s32[64,48]{0,1:T(8,128)}, u32[]{:S(2)}) copy-start(s32[64,48]{0,1:T(8,128)} %param.16) | copy-start | bytes 36868
  0.0 39.3 %collective-permute-start.1 = (bf16[25,64,128]{2,1,0:T(8,128)(2,1)}, bf16[25,64,128]{2,1,0:T(8,128)(2,1)}, u32[]{:S(2)}, u32[]{:S(2)}) collective-permute-start(bf16[25,64,128]{2,1,0:T(8,128)(2,1)} %bitcast.18), channel_id=1, source_target_pairs={{1,0},{2,1},{3,2},{4,3},{5,4},{6,5},{7,6},{8,7},{9,8},{10,9},{11,1... | collective-permute-start | bytes 1228808 | tf_op jit(solution)/shard_map/ppermute | solution.py:404
  11.4 13.4 %all-to-all-start = ((bf16[16,88,128]{2,1,0:T(8,128)(2,1)}), bf16[16,88,128]{2,1,0:T(8,128)(2,1)S(1)}, u32[]{:S(2)}, u32[]{:S(2)}) async-start(bf16[16,88,128]{2,1,0:T(8,128)(2,1)} %bitcast.21), calls=%async_computation | async-start | bytes 720896 | tf_op jit(solution)/shard_map/all_to_all | solution.py:380
  17.9 21.5 %collective-permute-start = (bf16[25,64,128]{2,1,0:T(8,128)(2,1)S(1)}, bf16[25,64,128]{2,1,0:T(8,128)(2,1)}, u32[]{:S(2)}, u32[]{:S(2)}) collective-permute-start(bf16[25,64,128]{2,1,0:T(8,128)(2,1)S(1)} %bitcast.19), channel_id=1, source_target_pairs={{0,1},{1,2},{2,3},{3,4},{4,5},{5,6},{6,7},{7,8},{8,9},{9,10},{10,1... | collective-permute-start | bytes 1228808 | tf_op jit(solution)/shard_map/ppermute | solution.py:403
  26.2 4.8 %copy-start = (bf16[64,48,165]{2,1,0:T(8,128)(2,1)S(1)}, bf16[64,48,165]{2,1,0:T(8,128)(2,1)}, u32[]{:S(2)}) copy-start(bf16[64,48,165]{2,1,0:T(8,128)(2,1)} %param.14) | copy-start | bytes 3041284
  26.2 27.6 %all-to-all-start.1 = ((bf16[64,88,128]{2,1,0:T(8,128)(2,1)}), bf16[64,88,128]{2,1,0:T(8,128)(2,1)S(1)}, u32[]{:S(2)}, u32[]{:S(2)}) async-start(bf16[64,88,128]{2,1,0:T(8,128)(2,1)} %broadcast_in_dim.16), calls=%async_computation.1 | async-start | bytes 2883584 | tf_op jit(solution)/shard_map/all_to_all | solution.py:383
  31.0 1.1 %copy-start.1 = (bf16[64,48,128]{2,1,0:T(8,128)(2,1)S(1)}, bf16[64,48,128]{2,1,0:T(8,128)(2,1)}, u32[]{:S(2)}) copy-start(bf16[64,48,128]{2,1,0:T(8,128)(2,1)} %param.15) | copy-start | bytes 2359300
  53.8 4.0 %collective-permute-start.2 = (bf16[5632,128]{1,0:T(8,128)(2,1)S(1)}, bf16[5632,128]{1,0:T(8,128)(2,1)S(1)}, u32[]{:S(2)}, u32[]{:S(2)}) collective-permute-start(bf16[5632,128]{1,0:T(8,128)(2,1)S(1)} %bitcast.12), channel_id=1, source_target_pairs={{0,8},{8,0},{1,9},{9,1},{2,10},{10,2},{3,11},{11,3},{4,12},{12,4},... | collective-permute-start | bytes 4325384 | tf_op jit(solution)/shard_map/ppermute | solution.py:408

commit v5 on v4

--- a/solution.py
+++ b/solution.py
@@ -260,11 +260,20 @@
     def _():
         place_weights(info[0], mine, other, mixes)
         total[...] = jnp.zeros_like(total)
-        gated[...] = jnp.zeros_like(gated)
-
-    @pl.when(step <= info[1])
-    def _():
-        mix_tile(step, rotated, frames, bounds, mixes, fresh, gated, message, spread, total)
+
+    refs = (step, rotated, frames, bounds, mixes, fresh, gated, message, spread, total)
+
+    @pl.when(step == 0)
+    def _():
+        mix_tile(True, False, *refs)
+
+    @pl.when(jnp.logical_and(step > 0, step < info[1]))
+    def _():
+        mix_tile(True, True, *refs)
+
+    @pl.when(step == info[1])
+    def _():
+        mix_tile(False, True, *refs)
 
     @pl.when(step == info[1])
     def _():
@@ -272,11 +281,12 @@
             out[q] = total[q * C : (q + 1) * C, :].T * scale[...]
 
 
-def mix_tile(step, rotated, frames, bounds, mixes, fresh, gated, message, spread, total):
+def mix_tile(mixing, turning, step, rotated, frames, bounds, mixes, fresh, gated, message, spread, total):
     edge = lax.broadcasted_iota(jnp.int32, (TILE, 64), 0) + (step - 1) * TILE
     owned = jnp.logical_and(edge >= bounds[0:1, :], edge < bounds[1:2, :])
     owner = owned.astype(jnp.float32).astype(jnp.bfloat16)
-    spread_frames(frames[0], spread)
+    if turning:
+        spread_frames(frames[0], spread)
 
     def mix_order(order, gate):
         begin = START[order] * C
@@ -319,17 +329,14 @@
         rows = slice(base * C, (base + size) * C)
         total[rows, :] += jnp.dot(message[rows, :], owner, preferred_element_type=jnp.float32)
 
-    gate = mix_order(0, None)
-    turn_back(4)
-    mix_order(1, gate)
-    turn_back(3)
-    mix_order(2, gate)
-    turn_back(2)
-    mix_order(3, gate)
-    turn_back(1)
-    mix_order(4, gate)
-    turn_back(0)
-    gated[...] = fresh[...]
+    gate = mix_order(0, None) if mixing else None
+    for degree, order in ((4, 1), (3, 2), (2, 3), (1, 4), (0, None)):
+        if turning:
+            turn_back(degree)
+        if mixing and order:
+            mix_order(order, gate)
+    if mixing:
+        gated[...] = fresh[...]
 
 
 def mix(info, mine, other, rotated, frames, bounds, scale):

time: 82.1 us -> 80 us (0.974)
  Pallas kernels: 49.4 us -> 47.4 us
    pallas_call x1, Pallas kernels: 24.2 us -> 22.2 us  [mix(): pl.pallas_call(mix_kernel, grid_spec=pltpu.PrefetchScalarGridSpec(num_sca...]
  transfers between devices with their start and end apart: 5 -> 5, of which waited for: 2 -> 2; matrix products, arithmetic and copies ran while one was open for 3% -> 3% of each run, Pallas kernels for 31% -> 32%
where the time goes in v5:
time: 80 us
  Pallas kernels  47.4 us (59%)
  starting transfers between devices  19.1 us (24%)
  waiting for transfers between devices  8.82 us (11%)
  local copies, waits for them, and re-layouts  2.83 us (4%)
  other arithmetic  1.17 us (1%)
    pallas_call x1, Pallas kernels, mix(): pl.pallas_call(mix_kernel, grid_spec=pltpu.PrefetchScalarGridSpec(num_sca...  22.2 us
    pallas_call x1, Pallas kernels, rotate(): pl.pallas_call(rotate_kernel, grid_spec=pltpu.PrefetchScalarGridSpec(num_...  14.5 us
    ppermute x1, starting transfers between devices, body(): lax.ppermute(node_features.transpose(1, 0, 2), ATOM_AXES, [(b, a) for a,...  7.86 us
    pallas_call x1, Pallas kernels, compact(): pl.pallas_call(compact_kernel, grid_spec=pltpu.PrefetchScalarGridSpec(num...  7.15 us
    all_to_all x1, waiting for transfers between devices, body(): lax.all_to_all(partial.reshape(-1, share_rows, C), ('core', 'x', 'yl'), 0...  6.05 us
    all_to_all x1, starting transfers between devices, body(): lax.all_to_all(partial.reshape(-1, share_rows, C), ('core', 'x', 'yl'), 0...  5.25 us
    all_to_all x1, starting transfers between devices, body(): mine = lax.all_to_all(copies, SAME_CORE, 0, 0, tiled=True).reshape(-1, C)  4.8 us
    pallas_call x1, Pallas kernels, combine(): pl.pallas_call(combine_kernel, grid_spec=pltpu.PrefetchScalarGridSpec(num...  3.56 us
  transfers between devices with their start and end apart: 5, of which 2 were waited for; matrix products, arithmetic and copies ran while one was open for 3% of the time, Pallas kernels for 32%

profile of v5, /device:TPU:1, one launch (start us, length us, event | category | flops | bytes accessed | tf_op | source)
XLA Modules:
  0.0 80.0 jit_solution(14667614445673632022)
XLA Ops:
  0.0 0.0 copy-start.3
  0.0 0.0 copy-start.5
  0.0 0.0 copy-start.2
  0.0 0.0 copy-start.4
  0.0 7.9 %collective-permute-start.1 = (bf16[25,64,128]{2,1,0:T(8,128)(2,1)}, bf16[25,64,128]{2,1,0:T(8,128)(2,1)}, u32[]{:S(2)}, u32[]{:S(2)}) collective-permute-start(bf16[25,64,128]{2,1,0:T(8,128)(2,1)} %bitcast.18), channel_id=1, source_target_pairs={{1,0},{2,1},{3,2},{4,3},{5,4},{6,5},{7,6},{8,7},{9,8},{10,9},{11,1... | collective-permute-start | bytes 1228808 | tf_op jit(solution)/shard_map/ppermute | solution.py:411
  7.9 3.6 %merge_group.1 = bf16[2,704,128]{2,1,0:T(8,128)(2,1)} custom-call(s32[352]{0:T(512)} %constant.109.clone.table, f32[2]{0:T(128)} %coeff.1, bf16[2,640,640]{2,1,0:T(8,128)(2,1)} %w0.1, bf16[2,2,512,512]{3,2,1,0:T(8,128)(2,1)} %w1.1, bf16[2,2,384,384]{3,2,1,0:T(8,128)(2,1)} %w2.1, bf16[2,2,256,256]{3,2,1,0:T(8,128)(2,1)} %w3.1, bf16[2,2,128,128]{3,2,1,0:T(8,128)(2,1)} %w4.1), custom_call_target="tpu_custom_call" | custom-call | flops 720896 | bytes 1081344 | tf_op jit(solution)/shard_map/merge_group/pallas_call | solution.py:83
  11.4 5.2 %all-to-all-start = ((bf16[16,88,128]{2,1,0:T(8,128)(2,1)}), bf16[16,88,128]{2,1,0:T(8,128)(2,1)S(1)}, u32[]{:S(2)}, u32[]{:S(2)}) async-start(bf16[16,88,128]{2,1,0:T(8,128)(2,1)} %bitcast.21), calls=%async_computation | async-start | bytes 720896 | tf_op jit(solution)/shard_map/all_to_all | solution.py:387
  16.7 0.0 copy-done.3
  16.7 0.0 copy-done.5
  16.7 0.1 multiply_reduce_fusion
  16.8 0.7 fusion.6
  17.5 0.2 convert_reduce_fusion
  17.7 0.1 copy.20
  17.8 0.1 select_n.50
  17.9 0.0 copy-done.2
  17.9 0.1 collective-permute-start
  18.6 0.0 copy-done.4
  18.7 0.1 copy.21
  18.7 0.1 reshape.78
  18.8 6.0 %all-to-all-done = bf16[16,88,128]{2,1,0:T(8,128)(2,1)S(1)} async-done(((bf16[16,88,128]{2,1,0:T(8,128)(2,1)}), bf16[16,88,128]{2,1,0:T(8,128)(2,1)S(1)}, u32[]{:S(2)}, u32[]{:S(2)}) %all-to-all-start) | async-done | bytes 360480 | tf_op jit(solution)/shard_map/all_to_all | solution.py:387
  24.9 0.1 reduce_sum.40
  24.9 1.3 %broadcast_in_dim.16 = bf16[64,88,128]{2,1,0:T(8,128)(2,1)} broadcast(bf16[88,128]{1,0:T(8,128)(2,1)S(1)} %reduce_sum.40), dimensions={1,2} | broadcast | bytes 1464320 | tf_op jit(solution)/shard_map/broadcast_in_dim | solution.py:389
  26.2 0.0 copy-start
  26.2 4.8 %all-to-all-start.1 = ((bf16[64,88,128]{2,1,0:T(8,128)(2,1)}), bf16[64,88,128]{2,1,0:T(8,128)(2,1)S(1)}, u32[]{:S(2)}, u32[]{:S(2)}) async-start(bf16[64,88,128]{2,1,0:T(8,128)(2,1)} %broadcast_in_dim.16), calls=%async_computation.1 | async-start | bytes 2883584 | tf_op jit(solution)/shard_map/all_to_all | solution.py:390
  31.0 0.0 copy-done
  31.0 0.0 copy-start.1
  31.1 1.1 %copy-done.1 = bf16[64,48,128]{2,1,0:T(8,128)(2,1)S(1)} copy-done((bf16[64,48,128]{2,1,0:T(8,128)(2,1)S(1)}, bf16[64,48,128]{2,1,0:T(8,128)(2,1)}, u32[]{:S(2)}) %copy-start.1) | copy-done | bytes 786456
  32.2 7.2 %compact_edges.1 = (f32[12,168,256]{2,1,0:T(8,128)}, f32[12,128,256]{2,1,0:T(8,128)S(1)}) custom-call(s32[12]{0:T(128)S(1)} %fusion.5.first, s32[1]{0:T(128)} %bitcast.1.tiles, s32[24,1,128]{2,1,0:T(1,128)S(1)} %bitcast.14, s32[24,1,128]{2,1,0:T(1,128)S(1)} %bitcast.15, bf16[3072,165]{1,0:T(8,128)(2,1)S(1)} %bitcast.16, bf16[3072,128]{1,0:T(8,128)(2,1)S(1)} %bitcast.17), custom_call_target="tpu_custom_call" | custom-call | flops 20000000000 | bytes 40000000 | tf_op jit(solution)/shard_map/compact_edges/pallas_call | solution.py:137
  39.3 0.0 collective-permute-done.low
  39.3 0.0 collective-permute-done.1.high
  39.3 14.5 %gather_rotate.1.rotated = bf16[12,3200,256]{2,1,0:T(8,128)(2,1)} custom-call(s32[1]{0:T(128)} %bitcast.1.tiles, f32[12,168,256]{2,1,0:T(8,128)} %get-tuple-element.26.frames, f32[12,128,256]{2,1,0:T(8,128)S(1)} %get-tuple-element.21.radial, bf16[25,64,128]{2,1,0:T(8,128)(2,1)S(1)} %bitcast.20, bf16[25,64,128]{2,1,0:T(8,128)(2,1)} %collective-permute-done.low, ...), custom_call_target="tpu_custom_call" | custom-call | flops 10000000000 | bytes 40000000 | tf_op jit(solution)/shard_map/gather_rotate/pallas_call | solution.py:195
  53.8 0.0 all-to-all-done.1
  53.8 1.1 %collective-permute-start.2 = (bf16[5632,128]{1,0:T(8,128)(2,1)S(1)}, bf16[5632,128]{1,0:T(8,128)(2,1)S(1)}, u32[]{:S(2)}, u32[]{:S(2)}) collective-permute-start(bf16[5632,128]{1,0:T(8,128)(2,1)S(1)} %bitcast.12), channel_id=1, source_target_pairs={{0,8},{8,0},{1,9},{9,1},{2,10},{10,2},{3,11},{11,3},{4,12},{12,4},... | collective-permute-start | bytes 4325384 | tf_op jit(solution)/shard_map/ppermute | solution.py:415
  55.0 0.1 pad_add_fusion.1.info
  55.0 2.8 %collective-permute-done.2.other = bf16[5632,128]{1,0:T(8,128)(2,1)S(1)} collective-permute-done((bf16[5632,128]{1,0:T(8,128)(2,1)S(1)}, bf16[5632,128]{1,0:T(8,128)(2,1)S(1)}, u32[]{:S(2)}, u32[]{:S(2)}) %collective-permute-start.2) | collective-permute-done | bytes 1441824 | tf_op jit(solution)/shard_map/ppermute | solution.py:415
  57.8 0.1 broadcast_in_dim.19.scale
  57.9 22.2 %mix_messages.1 = f32[25,64,128]{2,1,0:T(8,128)} custom-call(s32[2]{0:T(128)S(1)} %pad_add_fusion.1.info, bf16[5632,128]{1,0:T(8,128)(2,1)S(1)} %bitcast.13, bf16[5632,128]{1,0:T(8,128)(2,1)S(1)} %collective-permute-done.2.other, bf16[12,3200,256]{2,1,0:T(8,128)(2,1)} %gather_rotate.1.rotated, f32[12,168,256]{2,1,0:T(8,128)} %get-tuple-element.26.frames, ...), custom_call_target="tpu_custom_call" | custom-call | flops 15000000512 | bytes 40000000 | tf_op jit(solution)/shard_map/mix_messages/pallas_call | solution.py:345
  (6 shorter events, 0.1 us)
Async XLA Ops:
  0.0 16.7 %copy-start.3 = (s32[64,64]{1,0:T(8,128)S(1)}, s32[64,64]{1,0:T(8,128)}, u32[]{:S(2)}) copy-start(s32[64,64]{1,0:T(8,128)} %constant.110.clone) | copy-start | bytes 49156
  0.0 16.7 %copy-start.5 = (s32[64]{0:T(128)S(1)}, s32[64]{0:T(128)}, u32[]{:S(2)}) copy-start(s32[64]{0:T(128)} %param.17) | copy-start | bytes 772
  0.0 17.9 %copy-start.2 = (bf16[64,25,128]{2,0,1:T(8,128)(2,1)S(1)}, bf16[64,25,128]{2,0,1:T(8,128)(2,1)}, u32[]{:S(2)}) copy-start(bf16[64,25,128]{2,0,1:T(8,128)(2,1)} %param.13) | copy-start | bytes 1228804
  0.0 18.6 %copy-start.4 = (s32[64,48]{0,1:T(8,128)S(1)}, s32[64,48]{0,1:T(8,128)}, u32[]{:S(2)}) copy-start(s32[64,48]{0,1:T(8,128)} %param.16) | copy-start | bytes 36868
  0.0 39.3 %collective-permute-start.1 = (bf16[25,64,128]{2,1,0:T(8,128)(2,1)}, bf16[25,64,128]{2,1,0:T(8,128)(2,1)}, u32[]{:S(2)}, u32[]{:S(2)}) collective-permute-start(bf16[25,64,128]{2,1,0:T(8,128)(2,1)} %bitcast.18), channel_id=1, source_target_pairs={{1,0},{2,1},{3,2},{4,3},{5,4},{6,5},{7,6},{8,7},{9,8},{10,9},{11,1... | collective-permute-start | bytes 1228808 | tf_op jit(solution)/shard_map/ppermute | solution.py:411
  11.4 13.4 %all-to-all-start = ((bf16[16,88,128]{2,1,0:T(8,128)(2,1)}), bf16[16,88,128]{2,1,0:T(8,128)(2,1)S(1)}, u32[]{:S(2)}, u32[]{:S(2)}) async-start(bf16[16,88,128]{2,1,0:T(8,128)(2,1)} %bitcast.21), calls=%async_computation | async-start | bytes 720896 | tf_op jit(solution)/shard_map/all_to_all | solution.py:387
  17.9 21.5 %collective-permute-start = (bf16[25,64,128]{2,1,0:T(8,128)(2,1)S(1)}, bf16[25,64,128]{2,1,0:T(8,128)(2,1)}, u32[]{:S(2)}, u32[]{:S(2)}) collective-permute-start(bf16[25,64,128]{2,1,0:T(8,128)(2,1)S(1)} %bitcast.19), channel_id=1, source_target_pairs={{0,1},{1,2},{2,3},{3,4},{4,5},{5,6},{6,7},{7,8},{8,9},{9,10},{10,1... | collective-permute-start | bytes 1228808 | tf_op jit(solution)/shard_map/ppermute | solution.py:410
  26.2 4.8 %copy-start = (bf16[64,48,165]{2,1,0:T(8,128)(2,1)S(1)}, bf16[64,48,165]{2,1,0:T(8,128)(2,1)}, u32[]{:S(2)}) copy-start(bf16[64,48,165]{2,1,0:T(8,128)(2,1)} %param.14) | copy-start | bytes 3041284
  26.2 27.6 %all-to-all-start.1 = ((bf16[64,88,128]{2,1,0:T(8,128)(2,1)}), bf16[64,88,128]{2,1,0:T(8,128)(2,1)S(1)}, u32[]{:S(2)}, u32[]{:S(2)}) async-start(bf16[64,88,128]{2,1,0:T(8,128)(2,1)} %broadcast_in_dim.16), calls=%async_computation.1 | async-start | bytes 2883584 | tf_op jit(solution)/shard_map/all_to_all | solution.py:390
  31.0 1.1 %copy-start.1 = (bf16[64,48,128]{2,1,0:T(8,128)(2,1)S(1)}, bf16[64,48,128]{2,1,0:T(8,128)(2,1)}, u32[]{:S(2)}) copy-start(bf16[64,48,128]{2,1,0:T(8,128)(2,1)} %param.15) | copy-start | bytes 2359300
  53.8 4.0 %collective-permute-start.2 = (bf16[5632,128]{1,0:T(8,128)(2,1)S(1)}, bf16[5632,128]{1,0:T(8,128)(2,1)S(1)}, u32[]{:S(2)}, u32[]{:S(2)}) collective-permute-start(bf16[5632,128]{1,0:T(8,128)(2,1)S(1)} %bitcast.12), channel_id=1, source_target_pairs={{0,8},{8,0},{1,9},{9,1},{2,10},{10,2},{3,11},{11,3},{4,12},{12,4},... | collective-permute-start | bytes 4325384 | tf_op jit(solution)/shard_map/ppermute | solution.py:415

commit v6 on v5

--- a/solution.py
+++ b/solution.py
@@ -74,7 +74,7 @@
     for j in range(BLOCKS_EACH):
         pltpu.make_async_copy(w0.at[:, pl.ds(0, C), pl.ds(0, C)], buf.at[j], sems.at[j]).wait()
         total = coeff[0] * buf[j, 0].astype(jnp.float32) + coeff[1] * buf[j, 1].astype(jnp.float32)
-        turned = total.T.astype(jnp.bfloat16)
+        turned = total.astype(jnp.bfloat16).T
         out[0, 64 * j : 64 * j + 64] = turned[:64]
         out[1, 64 * j : 64 * j + 64] = turned[64:]
 
@@ -217,9 +217,11 @@
     return (3, size // 2, size // 2) if order in THREE else (size, size)
 
 
-def place_weights(core, mine, other, mixes):
+def place_weights(which, core, mine, other, mixes):
     where = {block: g for g, block in enumerate(BLOCKS)}
     for g, (order, part, o, i) in enumerate(BLOCKS):
+        if order != which:
+            continue
         if order in THREE:
             if part == 0:
                 pair = where[order, 1, o, i]
@@ -258,22 +260,23 @@
 
     @pl.when(step == 0)
     def _():
-        place_weights(info[0], mine, other, mixes)
         total[...] = jnp.zeros_like(total)
 
     refs = (step, rotated, frames, bounds, mixes, fresh, gated, message, spread, total)
 
+    place = lambda order: place_weights(order, info[0], mine, other, mixes)
+
     @pl.when(step == 0)
     def _():
-        mix_tile(True, False, *refs)
+        mix_tile(place, True, False, *refs)
 
     @pl.when(jnp.logical_and(step > 0, step < info[1]))
     def _():
-        mix_tile(True, True, *refs)
+        mix_tile(None, True, True, *refs)
 
     @pl.when(step == info[1])
     def _():
-        mix_tile(False, True, *refs)
+        mix_tile(None, False, True, *refs)
 
     @pl.when(step == info[1])
     def _():
@@ -281,7 +284,7 @@
             out[q] = total[q * C : (q + 1) * C, :].T * scale[...]
 
 
-def mix_tile(mixing, turning, step, rotated, frames, bounds, mixes, fresh, gated, message, spread, total):
+def mix_tile(place, mixing, turning, step, rotated, frames, bounds, mixes, fresh, gated, message, spread, total):
     edge = lax.broadcasted_iota(jnp.int32, (TILE, 64), 0) + (step - 1) * TILE
     owned = jnp.logical_and(edge >= bounds[0:1, :], edge < bounds[1:2, :])
     owner = owned.astype(jnp.float32).astype(jnp.bfloat16)
@@ -329,10 +332,15 @@
         rows = slice(base * C, (base + size) * C)
         total[rows, :] += jnp.dot(message[rows, :], owner, preferred_element_type=jnp.float32)
 
+    if place:
+        place(0)
+        place(1)
     gate = mix_order(0, None) if mixing else None
     for degree, order in ((4, 1), (3, 2), (2, 3), (1, 4), (0, None)):
         if turning:
             turn_back(degree)
+        if place and order and order < 4:
+            place(order + 1)
         if mixing and order:
             mix_order(order, gate)
     if mixing:

time: 80 us -> 79.9 us (level)
  transfers between devices with their start and end apart: 5 -> 5, of which waited for: 2 -> 2; matrix products, arithmetic and copies ran while one was open for 3% -> 4% of each run, Pallas kernels for 32% -> 31%
where the time goes in v6:
time: 79.9 us; the launch traced here: 79.4 us
  Pallas kernels  46.8 us (59%)
  starting transfers between devices  19.1 us (24%)
  waiting for transfers between devices  8.82 us (11%)
  local copies, waits for them, and re-layouts  2.83 us (4%)
  other arithmetic  1.17 us (1%)
    pallas_call x1, Pallas kernels, mix(): pl.pallas_call(mix_kernel, grid_spec=pltpu.PrefetchScalarGridSpec(num_sca...  21.9 us
    pallas_call x1, Pallas kernels, rotate(): pl.pallas_call(rotate_kernel, grid_spec=pltpu.PrefetchScalarGridSpec(num_...  14.5 us
    ppermute x1, starting transfers between devices, body(): lax.ppermute(node_features.transpose(1, 0, 2), ATOM_AXES, [(b, a) for a,...  7.86 us
    pallas_call x1, Pallas kernels, compact(): pl.pallas_call(compact_kernel, grid_spec=pltpu.PrefetchScalarGridSpec(num...  7.15 us
    all_to_all x1, waiting for transfers between devices, body(): lax.all_to_all(partial.reshape(-1, share_rows, C), ('core', 'x', 'yl'), 0...  6.05 us
    all_to_all x1, starting transfers between devices, body(): lax.all_to_all(partial.reshape(-1, share_rows, C), ('core', 'x', 'yl'), 0...  5.25 us
    all_to_all x1, starting transfers between devices, body(): mine = lax.all_to_all(copies, SAME_CORE, 0, 0, tiled=True).reshape(-1, C)  4.8 us
    pallas_call x1, Pallas kernels, combine(): pl.pallas_call(combine_kernel, grid_spec=pltpu.PrefetchScalarGridSpec(num...  3.24 us
  transfers between devices with their start and end apart: 5, of which 2 were waited for; matrix products, arithmetic and copies ran while one was open for 4% of the time, Pallas kernels for 31%

profile of v6, /device:TPU:1, one launch (start us, length us, event | category | flops | bytes accessed | tf_op | source)
XLA Modules:
  0.0 79.4 jit_solution(6408147740663422395)
XLA Ops:
  0.0 0.0 copy-start.3
  0.0 0.0 copy-start.5
  0.0 0.0 copy-start.2
  0.0 0.0 copy-start.4
  0.0 7.9 %collective-permute-start.1 = (bf16[25,64,128]{2,1,0:T(8,128)(2,1)}, bf16[25,64,128]{2,1,0:T(8,128)(2,1)}, u32[]{:S(2)}, u32[]{:S(2)}) collective-permute-start(bf16[25,64,128]{2,1,0:T(8,128)(2,1)} %bitcast.18), channel_id=1, source_target_pairs={{1,0},{2,1},{3,2},{4,3},{5,4},{6,5},{7,6},{8,7},{9,8},{10,9},{11,1... | collective-permute-start | bytes 1228808 | tf_op jit(solution)/shard_map/ppermute | solution.py:419
  7.9 3.2 %merge_group.1 = bf16[2,704,128]{2,1,0:T(8,128)(2,1)} custom-call(s32[352]{0:T(512)} %constant.109.clone.table, f32[2]{0:T(128)} %coeff.1, bf16[2,640,640]{2,1,0:T(8,128)(2,1)} %w0.1, bf16[2,2,512,512]{3,2,1,0:T(8,128)(2,1)} %w1.1, bf16[2,2,384,384]{3,2,1,0:T(8,128)(2,1)} %w2.1, bf16[2,2,256,256]{3,2,1,0:T(8,128)(2,1)} %w3.1, bf16[2,2,128,128]{3,2,1,0:T(8,128)(2,1)} %w4.1), custom_call_target="tpu_custom_call" | custom-call | flops 720896 | bytes 1081344 | tf_op jit(solution)/shard_map/merge_group/pallas_call | solution.py:83
  11.1 5.2 %all-to-all-start = ((bf16[16,88,128]{2,1,0:T(8,128)(2,1)}), bf16[16,88,128]{2,1,0:T(8,128)(2,1)S(1)}, u32[]{:S(2)}, u32[]{:S(2)}) async-start(bf16[16,88,128]{2,1,0:T(8,128)(2,1)} %bitcast.21), calls=%async_computation | async-start | bytes 720896 | tf_op jit(solution)/shard_map/all_to_all | solution.py:395
  16.4 0.0 copy-done.3
  16.4 0.0 copy-done.5
  16.4 0.1 multiply_reduce_fusion
  16.5 0.7 fusion.6
  17.2 0.2 convert_reduce_fusion
  17.4 0.1 copy.20
  17.5 0.1 select_n.50
  17.5 0.0 copy-done.2
  17.5 0.1 collective-permute-start
  18.3 0.0 copy-done.4
  18.3 0.1 copy.21
  18.4 0.1 reshape.78
  18.5 6.0 %all-to-all-done = bf16[16,88,128]{2,1,0:T(8,128)(2,1)S(1)} async-done(((bf16[16,88,128]{2,1,0:T(8,128)(2,1)}), bf16[16,88,128]{2,1,0:T(8,128)(2,1)S(1)}, u32[]{:S(2)}, u32[]{:S(2)}) %all-to-all-start) | async-done | bytes 360480 | tf_op jit(solution)/shard_map/all_to_all | solution.py:395
  24.5 0.1 reduce_sum.40
  24.6 1.3 %broadcast_in_dim.16 = bf16[64,88,128]{2,1,0:T(8,128)(2,1)} broadcast(bf16[88,128]{1,0:T(8,128)(2,1)S(1)} %reduce_sum.40), dimensions={1,2} | broadcast | bytes 1464320 | tf_op jit(solution)/shard_map/broadcast_in_dim | solution.py:397
  25.9 0.0 copy-start
  25.9 4.8 %all-to-all-start.1 = ((bf16[64,88,128]{2,1,0:T(8,128)(2,1)}), bf16[64,88,128]{2,1,0:T(8,128)(2,1)S(1)}, u32[]{:S(2)}, u32[]{:S(2)}) async-start(bf16[64,88,128]{2,1,0:T(8,128)(2,1)} %broadcast_in_dim.16), calls=%async_computation.1 | async-start | bytes 2883584 | tf_op jit(solution)/shard_map/all_to_all | solution.py:398
  30.7 0.0 copy-done
  30.7 0.0 copy-start.1
  30.7 1.1 %copy-done.1 = bf16[64,48,128]{2,1,0:T(8,128)(2,1)S(1)} copy-done((bf16[64,48,128]{2,1,0:T(8,128)(2,1)S(1)}, bf16[64,48,128]{2,1,0:T(8,128)(2,1)}, u32[]{:S(2)}) %copy-start.1) | copy-done | bytes 786456
  31.9 7.2 %compact_edges.1 = (f32[12,168,256]{2,1,0:T(8,128)}, f32[12,128,256]{2,1,0:T(8,128)S(1)}) custom-call(s32[12]{0:T(128)S(1)} %fusion.5.first, s32[1]{0:T(128)} %bitcast.1.tiles, s32[24,1,128]{2,1,0:T(1,128)S(1)} %bitcast.14, s32[24,1,128]{2,1,0:T(1,128)S(1)} %bitcast.15, bf16[3072,165]{1,0:T(8,128)(2,1)S(1)} %bitcast.16, bf16[3072,128]{1,0:T(8,128)(2,1)S(1)} %bitcast.17), custom_call_target="tpu_custom_call" | custom-call | flops 20000000000 | bytes 40000000 | tf_op jit(solution)/shard_map/compact_edges/pallas_call | solution.py:137
  39.0 0.0 collective-permute-done.low
  39.0 0.0 collective-permute-done.1.high
  39.0 14.5 %gather_rotate.1.rotated = bf16[12,3200,256]{2,1,0:T(8,128)(2,1)} custom-call(s32[1]{0:T(128)} %bitcast.1.tiles, f32[12,168,256]{2,1,0:T(8,128)} %get-tuple-element.26.frames, f32[12,128,256]{2,1,0:T(8,128)S(1)} %get-tuple-element.21.radial, bf16[25,64,128]{2,1,0:T(8,128)(2,1)S(1)} %bitcast.20, bf16[25,64,128]{2,1,0:T(8,128)(2,1)} %collective-permute-done.low, ...), custom_call_target="tpu_custom_call" | custom-call | flops 10000000000 | bytes 40000000 | tf_op jit(solution)/shard_map/gather_rotate/pallas_call | solution.py:195
  53.5 0.0 all-to-all-done.1
  53.5 1.1 %collective-permute-start.2 = (bf16[5632,128]{1,0:T(8,128)(2,1)S(1)}, bf16[5632,128]{1,0:T(8,128)(2,1)S(1)}, u32[]{:S(2)}, u32[]{:S(2)}) collective-permute-start(bf16[5632,128]{1,0:T(8,128)(2,1)S(1)} %bitcast.12), channel_id=1, source_target_pairs={{0,8},{8,0},{1,9},{9,1},{2,10},{10,2},{3,11},{11,3},{4,12},{12,4},... | collective-permute-start | bytes 4325384 | tf_op jit(solution)/shard_map/ppermute | solution.py:423
  54.6 0.1 pad_add_fusion.1.info
  54.7 2.8 %collective-permute-done.2.other = bf16[5632,128]{1,0:T(8,128)(2,1)S(1)} collective-permute-done((bf16[5632,128]{1,0:T(8,128)(2,1)S(1)}, bf16[5632,128]{1,0:T(8,128)(2,1)S(1)}, u32[]{:S(2)}, u32[]{:S(2)}) %collective-permute-start.2) | collective-permute-done | bytes 1441824 | tf_op jit(solution)/shard_map/ppermute | solution.py:423
  57.5 0.1 broadcast_in_dim.19.scale
  57.5 21.9 %mix_messages.1 = f32[25,64,128]{2,1,0:T(8,128)} custom-call(s32[2]{0:T(128)S(1)} %pad_add_fusion.1.info, bf16[5632,128]{1,0:T(8,128)(2,1)S(1)} %bitcast.13, bf16[5632,128]{1,0:T(8,128)(2,1)S(1)} %collective-permute-done.2.other, bf16[12,3200,256]{2,1,0:T(8,128)(2,1)} %gather_rotate.1.rotated, f32[12,168,256]{2,1,0:T(8,128)} %get-tuple-element.26.frames, ...), custom_call_target="tpu_custom_call" | custom-call | flops 15000000512 | bytes 40000000 | tf_op jit(solution)/shard_map/mix_messages/pallas_call | solution.py:353
  (6 shorter events, 0.1 us)
Async XLA Ops:
  0.0 16.4 %copy-start.3 = (s32[64,64]{1,0:T(8,128)S(1)}, s32[64,64]{1,0:T(8,128)}, u32[]{:S(2)}) copy-start(s32[64,64]{1,0:T(8,128)} %constant.110.clone) | copy-start | bytes 49156
  0.0 16.4 %copy-start.5 = (s32[64]{0:T(128)S(1)}, s32[64]{0:T(128)}, u32[]{:S(2)}) copy-start(s32[64]{0:T(128)} %param.17) | copy-start | bytes 772
  0.0 17.5 %copy-start.2 = (bf16[64,25,128]{2,0,1:T(8,128)(2,1)S(1)}, bf16[64,25,128]{2,0,1:T(8,128)(2,1)}, u32[]{:S(2)}) copy-start(bf16[64,25,128]{2,0,1:T(8,128)(2,1)} %param.13) | copy-start | bytes 1228804
  0.0 18.3 %copy-start.4 = (s32[64,48]{0,1:T(8,128)S(1)}, s32[64,48]{0,1:T(8,128)}, u32[]{:S(2)}) copy-start(s32[64,48]{0,1:T(8,128)} %param.16) | copy-start | bytes 36868
  0.0 39.0 %collective-permute-start.1 = (bf16[25,64,128]{2,1,0:T(8,128)(2,1)}, bf16[25,64,128]{2,1,0:T(8,128)(2,1)}, u32[]{:S(2)}, u32[]{:S(2)}) collective-permute-start(bf16[25,64,128]{2,1,0:T(8,128)(2,1)} %bitcast.18), channel_id=1, source_target_pairs={{1,0},{2,1},{3,2},{4,3},{5,4},{6,5},{7,6},{8,7},{9,8},{10,9},{11,1... | collective-permute-start | bytes 1228808 | tf_op jit(solution)/shard_map/ppermute | solution.py:419
  11.1 13.4 %all-to-all-start = ((bf16[16,88,128]{2,1,0:T(8,128)(2,1)}), bf16[16,88,128]{2,1,0:T(8,128)(2,1)S(1)}, u32[]{:S(2)}, u32[]{:S(2)}) async-start(bf16[16,88,128]{2,1,0:T(8,128)(2,1)} %bitcast.21), calls=%async_computation | async-start | bytes 720896 | tf_op jit(solution)/shard_map/all_to_all | solution.py:395
  17.5 21.5 %collective-permute-start = (bf16[25,64,128]{2,1,0:T(8,128)(2,1)S(1)}, bf16[25,64,128]{2,1,0:T(8,128)(2,1)}, u32[]{:S(2)}, u32[]{:S(2)}) collective-permute-start(bf16[25,64,128]{2,1,0:T(8,128)(2,1)S(1)} %bitcast.19), channel_id=1, source_target_pairs={{0,1},{1,2},{2,3},{3,4},{4,5},{5,6},{6,7},{7,8},{8,9},{9,10},{10,1... | collective-permute-start | bytes 1228808 | tf_op jit(solution)/shard_map/ppermute | solution.py:418
  25.9 4.8 %copy-start = (bf16[64,48,165]{2,1,0:T(8,128)(2,1)S(1)}, bf16[64,48,165]{2,1,0:T(8,128)(2,1)}, u32[]{:S(2)}) copy-start(bf16[64,48,165]{2,1,0:T(8,128)(2,1)} %param.14) | copy-start | bytes 3041284
  25.9 27.6 %all-to-all-start.1 = ((bf16[64,88,128]{2,1,0:T(8,128)(2,1)}), bf16[64,88,128]{2,1,0:T(8,128)(2,1)S(1)}, u32[]{:S(2)}, u32[]{:S(2)}) async-start(bf16[64,88,128]{2,1,0:T(8,128)(2,1)} %broadcast_in_dim.16), calls=%async_computation.1 | async-start | bytes 2883584 | tf_op jit(solution)/shard_map/all_to_all | solution.py:398
  30.7 1.1 %copy-start.1 = (bf16[64,48,128]{2,1,0:T(8,128)(2,1)S(1)}, bf16[64,48,128]{2,1,0:T(8,128)(2,1)}, u32[]{:S(2)}) copy-start(bf16[64,48,128]{2,1,0:T(8,128)(2,1)} %param.15) | copy-start | bytes 2359300
  53.5 4.0 %collective-permute-start.2 = (bf16[5632,128]{1,0:T(8,128)(2,1)S(1)}, bf16[5632,128]{1,0:T(8,128)(2,1)S(1)}, u32[]{:S(2)}, u32[]{:S(2)}) collective-permute-start(bf16[5632,128]{1,0:T(8,128)(2,1)S(1)} %bitcast.12), channel_id=1, source_target_pairs={{0,8},{8,0},{1,9},{9,1},{2,10},{10,2},{3,11},{11,3},{4,12},{12,4},... | collective-permute-start | bytes 4325384 | tf_op jit(solution)/shard_map/ppermute | solution.py:423
